TPU v7x, 32 devices: a whole 2x2x4 slice. The times are simulated.
32 devices in a mesh: row: 4 (over y, x), col: 8 (over z, core).
Axes of the slice: x: 2, y: 2, z: 4, core: 2. Of those that a mesh axis runs over, the one named last changes fastest.
Arguments:
- attributes: bfloat16 [16384, 128], P(('row', 'col')), may hold values from -6 to 6
- adj_values: bfloat16 [4, 8, 192, 128, 128], P('row', 'col'), may hold values from 0 to 3, as said below
- adj_rows: int32 [4, 8, 192], P('row', 'col'), may hold values from 0 to 31
- adj_cols: int32 [4, 8, 192], P('row', 'col'), may hold values from 0 to 15
- adj_count: int32 [4, 8], P('row', 'col'), may hold values from 1 to 192, as said below
- pair_ids: int32 [128, 4], P(('row', 'col')), may hold values from 0 to 15
- struct_target: bfloat16 [16384, 4, 128], P(('row', 'col')), may hold values from 0 to 1
- w_first: bfloat16 [128, 512], replicated, may hold values from -0.5 to 0.5
- w_rest: bfloat16 [1, 256, 512], replicated, may hold values from -0.375 to 0.375
- layer_bias: float32 [1, 256], replicated, may hold values from -3 to 3
- w_attr: bfloat16 [256, 128], replicated, may hold values from -0.375 to 0.375
- attr_bias: float32 [128], replicated, may hold values from -3 to 3
Outputs:
- anomaly: float32 [16384], P(('row', 'col'))
Inputs may be any that keep to these rules, and one draw needn't show every extreme that they name: `adj_count`: every tile has at least one live slot, and some tile has all 192 live in every draw. `adj_values`: nonnegative entries; slots at or past a tile's count are ignored.
All inputs are finite; a program needn't handle non-finite values.
Results may differ from a plain program's by a relative error of at most 0.00075.
Values may be sent and summed in bfloat16 or wider, within the bound.
A program may use at most 128 MiB of HBM per device.

v0:
```python
import math

import jax
import jax.numpy as jnp
from jax import lax
from jax.sharding import PartitionSpec as P

epsilon = 1e-06
mix_alpha = 0.8


def run_blocks(partial_sum, panel_blocks, block_vals, row_ids, col_ids, low_slot, high_slot):
    capacity = block_vals.shape[0]
    group_size = math.gcd(capacity, 32)

    def add_group(group_index, carried):
        start = group_index * group_size
        vals_now = lax.dynamic_slice_in_dim(block_vals, start, group_size, 0)
        rows_now = lax.dynamic_slice_in_dim(row_ids, start, group_size, 0)
        cols_now = lax.dynamic_slice_in_dim(col_ids, start, group_size, 0)
        slot_ids = start + jnp.arange(group_size, dtype=jnp.int32)
        live_mask = ((slot_ids >= low_slot) & (slot_ids < high_slot)).astype(jnp.float32)
        picked = jnp.take(panel_blocks, cols_now, axis=0)
        products = jnp.einsum("gij,gjf->gif", vals_now, picked, preferred_element_type=jnp.float32)
        return carried.at[rows_now].add(products * live_mask[:, None, None])

    first_group = low_slot // group_size
    last_group = (high_slot + group_size - 1) // group_size
    return lax.fori_loop(first_group, last_group, add_group, partial_sum)


def column_panel(features):
    gathered = lax.all_gather(features, "row", axis=0, tiled=True)
    return gathered


def per_device(
    attributes,
    adj_values,
    adj_rows,
    adj_cols,
    adj_count,
    pair_ids,
    struct_target,
    w_first,
    w_rest,
    layer_bias,
    w_attr,
    attr_bias,
):
    block_vals = adj_values[0, 0]
    row_ids = adj_rows[0, 0]
    col_ids = adj_cols[0, 0]
    live_count = adj_count[0, 0]
    capacity = block_vals.shape[0]
    block_size = block_vals.shape[1]
    nodes_dev = attributes.shape[0]
    hidden_size = w_rest.shape[1]
    pair_count = pair_ids.shape[1]
    row_blocks = lax.axis_size("col") * nodes_dev // block_size
    slot_ids = jnp.arange(capacity, dtype=jnp.int32)
    live_mask = (slot_ids < live_count).astype(jnp.float32)
    row_mass = jnp.sum(block_vals, axis=2, dtype=jnp.float32) * live_mask[:, None]
    degree_terms = jnp.zeros((row_blocks, block_size), jnp.float32).at[row_ids].add(row_mass)
    degree = 1.0 + lax.psum_scatter(
        degree_terms.reshape(-1).astype(jnp.bfloat16), "col", scatter_dimension=0, tiled=True
    ).astype(jnp.float32)
    row_scale = lax.rsqrt(degree)[:, None]
    hidden_state = attributes
    for layer_index in range(w_rest.shape[0] + 1):
        weight = w_first if layer_index == 0 else w_rest[layer_index - 1]
        projected = jnp.dot(hidden_state, weight, preferred_element_type=jnp.float32)
        features = projected[:, :hidden_size].astype(jnp.bfloat16)
        panel_rows = column_panel(features)
        panel_blocks = panel_rows.reshape(-1, block_size, hidden_size)
        partial_sum = jnp.zeros((row_blocks, block_size, hidden_size), jnp.float32)
        partial_sum = run_blocks(
            partial_sum, panel_blocks, block_vals, row_ids, col_ids, jnp.int32(0), live_count
        )
        flattened = partial_sum.reshape(-1, hidden_size)
        summed = lax.psum_scatter(
            flattened.astype(jnp.bfloat16), "col", scatter_dimension=0, tiled=True
        ).astype(jnp.float32)
        before = row_scale * summed + projected[:, hidden_size:]
        if layer_index > 0:
            before = before + layer_bias[layer_index - 1]
        hidden_state = jnp.tanh(before).astype(jnp.bfloat16)
    rebuilt = jnp.dot(hidden_state, w_attr, preferred_element_type=jnp.float32) + attr_bias
    attr_error = jnp.sqrt(
        jnp.mean((rebuilt - attributes.astype(jnp.float32)) ** 2, axis=1) + epsilon
    )
    group_blocks = column_panel(hidden_state).reshape(-1, block_size, hidden_size)
    own_blocks = hidden_state.reshape(-1, block_size, hidden_size)
    partners = jnp.take(group_blocks, pair_ids, axis=0)
    logits = jnp.einsum(
        "bif,bpjf->bipj", own_blocks, partners, preferred_element_type=jnp.float32
    ) * hidden_size ** (-0.5)
    probability = jax.nn.sigmoid(logits).reshape(nodes_dev, pair_count, block_size)
    struct_error = jnp.sqrt(
        jnp.mean((probability - struct_target.astype(jnp.float32)) ** 2, axis=(1, 2)) + epsilon
    )
    return mix_alpha * attr_error + (1.0 - mix_alpha) * struct_error


def solution(mesh):
    return jax.shard_map(
        per_device,
        mesh=mesh,
        in_specs=(
            P(("row", "col"), None),
            P("row", "col", None, None, None),
            P("row", "col", None),
            P("row", "col", None),
            P("row", "col"),
            P(("row", "col"), None),
            P(("row", "col"), None, None),
            P(),
            P(),
            P(),
            P(),
            P(),
        ),
        out_specs=P(("row", "col")),
        check_vma=False,
    )
```

profile of v0, /device:TPU:0, one launch (start us, length us, event | category | flops | bytes accessed | tf_op | source)
XLA Modules:
  0.0 375.3 jit_solution(11761909586776683755)
XLA Ops:
  6.5 1.3 fusion.38
  7.9 1.1 copy-done.3
  8.9 0.7 slice.44
  9.7 0.0 all-gather.4.cloned.1.call-update
  9.7 0.0 reduce-scatter.3.cloned.1.call-start
  10.4 28.8 %all-gather.4.cloned.1.call-done = bf16[2048,256]{1,0:T(8,128)(2,1)} async-done(((bf16[512,256]{1,0:T(8,128)(2,1)}), bf16[2048,256]{1,0:T(8,128)(2,1)}) %all-gather.4.cloned.1.call-update) | async-done | bytes 1048592 | tf_op jit(solution)/shard_map/all_gather | solution.py:33
  39.2 2.5 broadcast.83.clone
  41.6 0.0 copy-done.9
  41.6 30.8 %while.20 = (s32[]{:T(128)}, f32[32,128,256]{2,1,0:T(8,128)}, s32[]{:T(128)}, s32[192]{0:T(256)S(1)}, bf16[192,128,128]{2,1,0:T(8,128)(2,1)}, /*index=5*/s32[192...) while((s32[]{:T(128)}, f32[32,128,256]{2,1,0:T(8,128)}, ...), condition=%wide.region_5.7_spmd, body=%wide.region_3.6_spmd.sunk | while | flops 271582656 | bytes 24122744 | solution.py:29
  41.7 0.7 compare_and_fusion.5
  42.4 0.7 gather_fusion
  43.1 3.9 %convolution_multiply_fusion.5 = f32[32,128,256]{2,1,0:T(8,128)} fusion(bf16[32,128,256]{2,1,0:T(8,128)(2,1)S(1)} %gather_fusion, f32[32]{0:T(128)S(1)} %get-tuple-element.231, pred[32]{0:T(512)(128)(4,1)S(1)} %get-tuple-element.232, bf16[192,128,128]{2,1,0:T(8,128)(2,1)} %get-tuple-element.272, s32[]{:T(128)S(6)} %select_n.84), kind=kOutput, calls=%fused_computation.6.clone.1 | convolution fusion | flops 270532608 | bytes 7340196 | tf_op jit(solution)/shard_map/while/body/gij,gjf->gif/dot_general | solution.py:24
  47.0 0.1 compare_select_fusion.10
  47.1 9.8 %scatter_fusion = f32[32,128,256]{2,1,0:T(8,128)} fusion(f32[32,128,256]{2,1,0:T(8,128)} %get-tuple-element.257, s32[32]{0:T(128)S(1)} %compare_select_fusion.10, f32[32,128,256]{2,1,0:T(8,128)} %convolution_multiply_fusion.5), kind=kCustom, calls=%fused_computation.3.clone.1 | custom fusion | flops 1048576 | bytes 12583040 | tf_op jit(solution)/shard_map/while/body/scatter-add | solution.py:25
  56.9 0.7 compare_and_fusion.5
  57.6 0.7 gather_fusion
  58.3 3.9 %convolution_multiply_fusion.5 = f32[32,128,256]{2,1,0:T(8,128)} fusion(bf16[32,128,256]{2,1,0:T(8,128)(2,1)S(1)} %gather_fusion, f32[32]{0:T(128)S(1)} %get-tuple-element.231, pred[32]{0:T(512)(128)(4,1)S(1)} %get-tuple-element.232, bf16[192,128,128]{2,1,0:T(8,128)(2,1)} %get-tuple-element.272, s32[]{:T(128)S(6)} %select_n.84), kind=kOutput, calls=%fused_computation.6.clone.1 | convolution fusion | flops 270532608 | bytes 7340196 | tf_op jit(solution)/shard_map/while/body/gij,gjf->gif/dot_general | solution.py:24
  62.3 0.1 compare_select_fusion.10
  62.3 10.1 %scatter_fusion = f32[32,128,256]{2,1,0:T(8,128)} fusion(f32[32,128,256]{2,1,0:T(8,128)} %get-tuple-element.257, s32[32]{0:T(128)S(1)} %compare_select_fusion.10, f32[32,128,256]{2,1,0:T(8,128)} %convolution_multiply_fusion.5), kind=kCustom, calls=%fused_computation.3.clone.1 | custom fusion | flops 1048576 | bytes 12583040 | tf_op jit(solution)/shard_map/while/body/scatter-add | solution.py:25
  72.4 3.8 %convert_element_type.70 = bf16[32,128,256]{2,1,0:T(8,128)(2,1)} convert(f32[32,128,256]{2,1,0:T(8,128)} %get-tuple-element.92) | non-fusion elementwise | flops 1048576 | bytes 6291456 | tf_op jit(solution)/shard_map/convert_element_type | solution.py:82
  76.3 0.0 reduce-scatter.3.cloned.1.call-update
  76.3 0.0 all-gather.6.cloned.1.call-start
  76.4 0.6 dynamic-slice
  77.6 4.5 %convert_reduce_fusion = f32[192,128]{1,0:T(8,128)S(1)} fusion(bf16[1,1,192,128,128]{4,3,2,1,0:T(8,128)(2,1)} %bitcast.42), kind=kLoop, calls=%fused_computation.30 | loop fusion | flops 6266880 | bytes 6389760 | tf_op jit(solution)/shard_map/reduce_sum | solution.py:63
  82.1 1.3 scatter_custom_fusion.2
  83.5 75.8 %all-reduce = bf16[4096]{0:T(1024)(128)(2,1)S(1)} all-reduce(bf16[4096]{0:T(1024)(128)(2,1)S(1)} %convert_bitcast_fusion), channel_id=2, replica_groups=mesh['row'=4,'col'=8] {'col'}, use_global_device_ids=true, to_apply=%region_2.0.clone | all-reduce | flops 4096 | bytes 16384
  159.2 0.1 add_rsqrt_fusion
  159.3 14.5 %reduce-scatter.3.cloned.1.call-done = bf16[512,256]{1,0:T(8,128)(2,1)} async-done(((bf16[4096,256]{1,0:T(8,128)(2,1)}), bf16[512,256]{1,0:T(8,128)(2,1)}) %reduce-scatter.3.cloned.1.call-update) | async-done | bytes 262160 | tf_op jit(solution)/shard_map/reduce_scatter | solution.py:81
  173.8 1.3 fusion.29
  175.1 1.1 copy-done.5
  176.1 0.7 slice.43
  176.9 0.0 all-gather.6.cloned.1.call-update
  176.9 0.0 reduce-scatter.5.cloned.1.call-start
  177.0 25.5 %all-gather.6.cloned.1.call-done = bf16[2048,256]{1,0:T(8,128)(2,1)} async-done(((bf16[512,256]{1,0:T(8,128)(2,1)}), bf16[2048,256]{1,0:T(8,128)(2,1)}) %all-gather.6.cloned.1.call-update) | async-done | bytes 1048592 | tf_op jit(solution)/shard_map/all_gather | solution.py:33
  202.5 2.5 broadcast.83
  204.9 30.8 %while.21 = (s32[]{:T(128)}, f32[32,128,256]{2,1,0:T(8,128)}, s32[]{:T(128)}, s32[192]{0:T(256)S(1)}, bf16[192,128,128]{2,1,0:T(8,128)(2,1)}, /*index=5*/s32[192...) while((s32[]{:T(128)}, f32[32,128,256]{2,1,0:T(8,128)}, ...), condition=%wide.region_9.11_spmd, body=%wide.region_7.10_spmd.sunk | while | flops 271582656 | bytes 24122744 | solution.py:29
  204.9 0.7 compare_and_fusion.6
  205.7 0.7 gather_fusion.1
  206.4 3.9 %convolution_multiply_fusion.6 = f32[32,128,256]{2,1,0:T(8,128)} fusion(bf16[32,128,256]{2,1,0:T(8,128)(2,1)S(1)} %gather_fusion.1, f32[32]{0:T(128)S(1)} %get-tuple-element.242, pred[32]{0:T(512)(128)(4,1)S(1)} %get-tuple-element.243, bf16[192,128,128]{2,1,0:T(8,128)(2,1)} %get-tuple-element.308, s32[]{:T(128)S(6)} %select_n.87), kind=kOutput, calls=%fused_computation.18.clone.1 | convolution fusion | flops 270532608 | bytes 7340196 | tf_op jit(solution)/shard_map/while/body/gij,gjf->gif/dot_general | solution.py:24
  210.3 0.1 compare_select_fusion.11
  210.4 9.8 %scatter_fusion.1 = f32[32,128,256]{2,1,0:T(8,128)} fusion(f32[32,128,256]{2,1,0:T(8,128)} %get-tuple-element.293, s32[32]{0:T(128)S(1)} %compare_select_fusion.11, f32[32,128,256]{2,1,0:T(8,128)} %convolution_multiply_fusion.6), kind=kCustom, calls=%fused_computation.4.clone.1 | custom fusion | flops 1048576 | bytes 12583040 | tf_op jit(solution)/shard_map/while/body/scatter-add | solution.py:25
  220.2 0.7 compare_and_fusion.6
  220.9 0.7 gather_fusion.1
  221.6 3.9 %convolution_multiply_fusion.6 = f32[32,128,256]{2,1,0:T(8,128)} fusion(bf16[32,128,256]{2,1,0:T(8,128)(2,1)S(1)} %gather_fusion.1, f32[32]{0:T(128)S(1)} %get-tuple-element.242, pred[32]{0:T(512)(128)(4,1)S(1)} %get-tuple-element.243, bf16[192,128,128]{2,1,0:T(8,128)(2,1)} %get-tuple-element.308, s32[]{:T(128)S(6)} %select_n.87), kind=kOutput, calls=%fused_computation.18.clone.1 | convolution fusion | flops 270532608 | bytes 7340196 | tf_op jit(solution)/shard_map/while/body/gij,gjf->gif/dot_general | solution.py:24
  225.6 0.1 compare_select_fusion.11
  225.6 10.1 %scatter_fusion.1 = f32[32,128,256]{2,1,0:T(8,128)} fusion(f32[32,128,256]{2,1,0:T(8,128)} %get-tuple-element.293, s32[32]{0:T(128)S(1)} %compare_select_fusion.11, f32[32,128,256]{2,1,0:T(8,128)} %convolution_multiply_fusion.6), kind=kCustom, calls=%fused_computation.4.clone.1 | custom fusion | flops 1048576 | bytes 12583040 | tf_op jit(solution)/shard_map/while/body/scatter-add | solution.py:25
  235.7 0.0 copy-start.13
  235.8 0.0 copy-start.14
  235.8 3.9 %convert_element_type.74 = bf16[32,128,256]{2,1,0:T(8,128)(2,1)} convert(f32[32,128,256]{2,1,0:T(8,128)} %get-tuple-element.93) | non-fusion elementwise | flops 1048576 | bytes 6291456 | tf_op jit(solution)/shard_map/convert_element_type | solution.py:82
  239.7 0.0 reduce-scatter.5.cloned.1.call-update
  239.7 0.0 all-gather.8.cloned.1.call-start
  239.8 97.3 %reduce-scatter.5.cloned.1.call-done = bf16[512,256]{1,0:T(8,128)(2,1)} async-done(((bf16[4096,256]{1,0:T(8,128)(2,1)}), bf16[512,256]{1,0:T(8,128)(2,1)}) %reduce-scatter.5.cloned.1.call-update) | async-done | bytes 262160 | tf_op jit(solution)/shard_map/reduce_scatter | solution.py:81
  337.1 1.8 fusion.25
  338.9 0.0 all-gather.8.cloned.1.call-update
  339.0 0.1 copy.17
  339.1 0.1 reshape.105
  339.2 1.2 fusion.18
  340.5 24.0 %all-gather.8.cloned.1.call-done = bf16[2048,256]{1,0:T(8,128)(2,1)} async-done(((bf16[512,256]{1,0:T(8,128)(2,1)}), bf16[2048,256]{1,0:T(8,128)(2,1)}) %all-gather.8.cloned.1.call-update) | async-done | bytes 1048592 | tf_op jit(solution)/shard_map/all_gather | solution.py:33
  364.4 1.8 gather_fusion.2
  366.3 0.0 copy-start.8
  366.3 1.6 fusion.15
  367.9 0.1 copy.18
  368.0 0.2 fusion.20
  368.2 0.6 multiply_add_fusion
  (37 shorter events, 0.1 us)
Async XLA Ops:
  6.5 167.2 %copy-start = (bf16[1,256,512]{2,1,0:T(8,128)(2,1)S(1)}, bf16[1,256,512]{2,1,0:T(8,128)(2,1)}, u32[]{:S(2)}) copy-start(bf16[1,256,512]{2,1,0:T(8,128)(2,1)} %param.26) | copy-start | bytes 786436
  6.5 35.1 %copy-start.12 = (s32[1,1,192]{2,1,0:T(1,128)S(1)}, s32[1,1,192]{2,1,0:T(1,128)}, u32[]{:S(2)}) copy-start(s32[1,1,192]{2,1,0:T(1,128)} %param.20) | copy-start | bytes 2308
  6.5 35.1 %copy-start.9 = (s32[1,1,192]{2,1,0:T(1,128)S(1)}, s32[1,1,192]{2,1,0:T(1,128)}, u32[]{:S(2)}) copy-start(s32[1,1,192]{2,1,0:T(1,128)} %param.21) | copy-start | bytes 2308
  6.5 32.6 %all-gather.4.cloned.1.call-start = ((), (), s32[]{:S(2)}) async-start(), calls=%async_computation.2 | async-start | bytes 1310720 | tf_op jit(solution)/shard_map/all_gather | solution.py:33
  7.8 1.1 copy-start.3
  9.7 164.1 %reduce-scatter.3.cloned.1.call-start = ((), (), s32[]{:S(2)}) async-start(), calls=%async_computation.3 | async-start | bytes 2359296 | tf_op jit(solution)/shard_map/reduce_scatter | solution.py:81
  39.2 2.5 copy-start.1
  72.4 3.9 %copy-start.15 = (u32[32]{0:T(128)S(1)}, u32[32]{0:T(128)}, u32[]{:S(2)}) copy-start(u32[32]{0:T(128)} %constant.110) | copy-start | bytes 388
  76.3 97.5 %copy-start.4 = (f32[512,512]{1,0:T(8,128)S(1)}, f32[512,512]{1,0:T(8,128)}, u32[]{:S(2)}) copy-start(f32[512,512]{1,0:T(8,128)} %copy-done.3) | copy-start | bytes 3145732
  76.3 126.2 %all-gather.6.cloned.1.call-start = ((), (), s32[]{:S(2)}) async-start(), calls=%async_computation.4 | async-start | bytes 1310720 | tf_op jit(solution)/shard_map/all_gather | solution.py:33
  175.1 1.1 copy-start.5
  176.9 160.2 %reduce-scatter.5.cloned.1.call-start = ((), (), s32[]{:S(2)}) async-start(), calls=%async_computation.5 | async-start | bytes 2359296 | tf_op jit(solution)/shard_map/reduce_scatter | solution.py:81
  202.5 2.5 copy-start.2
  235.7 101.4 %copy-start.6 = (f32[512,512]{1,0:T(8,128)S(1)}, f32[512,512]{1,0:T(8,128)}, u32[]{:S(2)}) copy-start(f32[512,512]{1,0:T(8,128)} %copy-done.5) | copy-start | bytes 3145732
  235.7 101.4 %copy-start.11 = (f32[1,256]{1,0:T(1,128)S(1)}, f32[1,256]{1,0:T(1,128)}, u32[]{:S(2)}) copy-start(f32[1,256]{1,0:T(1,128)} %param.27) | copy-start | bytes 3076
  235.7 103.2 %copy-start.7 = (bf16[512,128]{1,0:T(8,128)(2,1)S(1)}, bf16[512,128]{1,0:T(8,128)(2,1)}, u32[]{:S(2)}) copy-start(bf16[512,128]{1,0:T(8,128)(2,1)} %param.18) | copy-start | bytes 393220
  235.7 103.4 %copy-start.10 = (s32[4,4]{1,0:T(4,128)S(1)}, s32[4,4]{1,0:T(4,128)}, u32[]{:S(2)}) copy-start(s32[4,4]{1,0:T(4,128)} %param.23) | copy-start | bytes 196
  235.7 103.5 %copy-start.13 = (bf16[256,128]{1,0:T(8,128)(2,1)S(1)}, bf16[256,128]{1,0:T(8,128)(2,1)}, u32[]{:S(2)}) copy-start(bf16[256,128]{1,0:T(8,128)(2,1)} %param.28) | copy-start | bytes 196612
  235.8 103.5 %copy-start.14 = (f32[128]{0:T(128)S(1)}, f32[128]{0:T(128)}, u32[]{:S(2)}) copy-start(f32[128]{0:T(128)} %param.29) | copy-start | bytes 1540
  239.7 124.7 %all-gather.8.cloned.1.call-start = ((), (), s32[]{:S(2)}) async-start(), calls=%async_computation.6 | async-start | bytes 1310720 | tf_op jit(solution)/shard_map/all_gather | solution.py:33
  366.3 1.7 copy-start.8
Sparse Core Ops, SparseCore 0:
  9.8 29.3 all-gather.3
  76.4 97.3 reduce-scatter.2
  177.0 25.3 all-gather.5
  239.8 97.2 reduce-scatter.4
  339.1 25.3 all-gather.7
where the time goes:
time: 377 us; the launch traced here: 375 us
  waiting for transfers between devices  190 us (50%)
  blocking collectives  75.8 us (20%)
  other arithmetic  59.3 us (16%)
  matrix products  21.2 us (6%)
  between operations  14.7 us (4%)
  local copies, waits for them, and re-layouts  14 us (4%)
    reduce_scatter x2, waiting for transfers between devices, per_device(): lax.psum_scatter(flattened.astype(jnp.bfloat16), 'col', scatter_dimension...  112 us
    all_gather x3, waiting for transfers between devices, column_panel(): gathered = lax.all_gather(features, 'row', axis=0, tiled=True)  78.2 us
    unnamed x1, blocking collectives  75.8 us
    scatter-add x4, other arithmetic, add_group(): return carried.at[rows_now].add(products * live_mask[:, None, None])  39.8 us
    dot_general x4, matrix products, add_group(): jnp.einsum('gij,gjf->gif', vals_now, picked, preferred_element_type=jnp.f...  15.8 us
    convert_element_type x2, other arithmetic, per_device(): flattened.astype(jnp.bfloat16)  7.76 us
  transfers between devices with their start and end apart: 5, of which 5 were waited for; matrix products, arithmetic and copies ran while one was open for 2% of the time, Pallas kernels for 0%

commit v1 on v0

v1 whole, which is shorter than its diff:
```python
import functools

import jax
import jax.numpy as jnp
from jax import lax
from jax.experimental import pallas as pl
from jax.experimental.pallas import tpu as pltpu
from jax.sharding import PartitionSpec as P

epsilon = 1e-06
mix_alpha = 0.8
MESH = pl.DeviceIdType.MESH
F32 = jnp.float32
BF16 = jnp.bfloat16
SUBS = 2
DEG_ROWS = 16


def dense_kernel(part_blocks, rows_ref, cols_ref, count_ref, vals_ref, out_ref):
    part = pl.program_id(0)
    blk = vals_ref.shape[1]
    out_ref[...] = jnp.zeros_like(out_ref)

    def add_slot(k, carry):
        row = rows_ref[k] - part * part_blocks

        @pl.when((row >= 0) & (row < part_blocks))
        def _():
            where_r = pl.ds(pl.multiple_of(row * blk, blk), blk)
            where_c = pl.ds(pl.multiple_of(cols_ref[k] * blk, blk), blk)
            out_ref[where_r, where_c] = out_ref[where_r, where_c] + vals_ref[k]

        return carry

    lax.fori_loop(0, count_ref[0], add_slot, 0)


def dense_tile(vals, row_ids, col_ids, count, row_blocks, col_blocks):
    cap, blk, _ = vals.shape
    part_blocks = 8
    grid_spec = pltpu.PrefetchScalarGridSpec(
        num_scalar_prefetch=3,
        grid=(row_blocks // part_blocks,),
        in_specs=[
            pl.BlockSpec((cap, blk, blk), lambda i, *_: (0, 0, 0), pipeline_mode=pl.Buffered(1))
        ],
        out_specs=pl.BlockSpec((part_blocks * blk, col_blocks * blk), lambda i, *_: (i, 0)),
    )
    return pl.pallas_call(
        functools.partial(dense_kernel, part_blocks),
        grid_spec=grid_spec,
        out_shape=jax.ShapeDtypeStruct((row_blocks * blk, col_blocks * blk), vals.dtype),
        compiler_params=pltpu.CompilerParams(vmem_limit_bytes=48 * 1024 * 1024),
        name="dense_tile",
    )(row_ids, col_ids, count, vals)


def graph_kernel(
    n_row,
    n_col,
    x_ref,
    a_ref,
    pair_ref,
    target_ref,
    w1_ref,
    w2_ref,
    b2_ref,
    wa_ref,
    ba_ref,
    out_ref,
    panel1,
    panel2,
    panel3,
    abuf,
    own1,
    own2,
    tot1,
    tot2,
    h1_ref,
    scale_ref,
    attr_ref,
    sib_out1,
    sib_in1,
    hop_out1,
    left_in1,
    right_in1,
    sib_out2,
    sib_in2,
    hop_out2,
    left_in2,
    right_in2,
    a_sem,
    g_send,
    g_recv,
    sib_send,
    sib_recv,
    hop_send,
    left_recv,
    right_recv,
):
    my_row = lax.axis_index("row")
    my_col = lax.axis_index("col")
    chips = n_col // 2
    chip = my_col // 2
    core = my_col % 2
    nodes, f_in = x_ref.shape
    hid = w2_ref.shape[0]
    blk = panel3.shape[1]
    sub = nodes // SUBS
    sub_blocks = sub // blk
    dev_blocks = nodes // blk
    steps = SUBS * chips

    sibling = (my_row, chip * 2 + 1 - core)
    right = (my_row, my_col + 2)
    left = (my_row, my_col - 2)
    peers = [(lax.rem(my_row + d, n_row), my_col) for d in range(1, n_row)]
    has_left = chip > 0
    has_right = chip < chips - 1

    far = jnp.maximum(chip, chips - 1 - chip)
    near = chips - 1 - far
    toward = jnp.where(2 * chip < chips - 1, 1, -1)

    def place(i):
        part = i // chips
        s = i - part * chips
        s2 = s - (far - near)
        paired = chip + (near - s2 // 2) * (1 - 2 * (s2 % 2))
        dest = jnp.where(s < far - near, chip + toward * (far - s), paired)
        return part, dest

    eye = lax.broadcasted_iota(jnp.int32, (blk, blk), 0) == lax.broadcasted_iota(
        jnp.int32, (blk, blk), 1
    )

    def to_row(square):
        return jnp.sum(jnp.where(eye, square, 0.0), axis=0, keepdims=True)

    def to_col(row):
        return jnp.sum(jnp.where(eye, jnp.broadcast_to(row, (blk, blk)), 0.0), axis=1, keepdims=True)

    def fetch(i, slot):
        part, dest = place(i)
        copies = []
        for which in range(2):
            pick = core if which == 0 else 1 - core
            start = pl.multiple_of((dest * 2 + pick) * nodes + part * sub, sub)
            copies.append(
                pltpu.make_async_copy(
                    a_ref.at[pl.ds(start, sub), :], abuf.at[slot, which], a_sem.at[slot, which]
                )
            )
        return copies

    def remote(src, dst, send, recv, device):
        return pltpu.make_async_remote_copy(
            src_ref=src,
            dst_ref=dst,
            send_sem=send,
            recv_sem=recv,
            device_id=device,
            device_id_type=MESH,
        )

    for copy in fetch(0, 0):
        copy.start()

    barrier = pltpu.get_barrier_semaphore()
    for device in [sibling] + peers:
        pl.semaphore_signal(barrier, inc=1, device_id=device, device_id_type=MESH)

    @pl.when(has_left)
    def _():
        pl.semaphore_signal(barrier, inc=1, device_id=left, device_id_type=MESH)

    @pl.when(has_right)
    def _():
        pl.semaphore_signal(barrier, inc=1, device_id=right, device_id_type=MESH)

    panel1[:, :, f_in:] = jnp.ones((n_row, nodes, panel1.shape[2] - f_in), BF16)
    panel1[my_row, :, :f_in] = x_ref[...]

    pl.semaphore_wait(barrier, n_row + jnp.minimum(chip, 1) + jnp.minimum(chips - 1 - chip, 1))

    def part1(row, part):
        return panel1.at[row, pl.ds(part * sub, sub), pl.ds(0, f_in)]

    def part2(row, part):
        return panel2.at[row, pl.ds(part * sub, sub), :]

    def part3(row, part):
        return panel3.at[pl.ds(row * dev_blocks + part * sub_blocks, sub_blocks)]

    def share(stage, view, part):
        for d in range(1, n_row):
            remote(
                view(my_row, part),
                view(my_row, part),
                g_send.at[stage, d - 1, part],
                g_recv.at[stage, d - 1, part],
                peers[d - 1],
            ).start()

    def gathered(stage, view, sent):
        for part in range(SUBS):
            for d in range(1, n_row):
                source = lax.rem(my_row + n_row - d, n_row)
                copy = remote(
                    view(my_row if sent else source, part),
                    view(my_row if sent else source, part),
                    g_send.at[stage, d - 1, part],
                    g_recv.at[stage, d - 1, part],
                    peers[d - 1],
                )
                if sent:
                    copy.wait_send()
                else:
                    copy.wait_recv()

    for part in range(SUBS):
        share(0, part1, part)
    gathered(0, part1, False)

    def aggregate(layer, panel, own, tot, sib_out, sib_in, hop_out, left_in, right_in, finish):
        def product(slot, which):
            total = None
            for r in range(n_row):
                term = jnp.dot(
                    abuf[slot, which, :, r * nodes : (r + 1) * nodes],
                    panel[r],
                    preferred_element_type=F32,
                )
                total = term if total is None else total + term
            return total

        def store(dst, value):
            if layer == 1:
                dst[...] = value.astype(dst.dtype)
                return
            dst[:sub, :] = value[:, :f_in].astype(dst.dtype)
            lane = lax.broadcasted_iota(jnp.int32, (DEG_ROWS, blk), 0)
            degree = jnp.zeros((DEG_ROWS, blk), F32)
            for b in range(sub_blocks):
                row = to_row(value[b * blk : (b + 1) * blk, f_in : f_in + blk])
                degree = jnp.where(lane == b, jnp.broadcast_to(row, (DEG_ROWS, blk)), degree)
            dst[sub:, :] = degree.astype(dst.dtype)

        def sib_copy(at):
            return remote(
                sib_out.at[at], sib_in.at[at], sib_send.at[layer, at], sib_recv.at[layer, at], sibling
            )

        def right_copy(at, device):
            return remote(
                hop_out.at[at], left_in.at[at], hop_send.at[layer, at], left_recv.at[layer, at], device
            )

        def left_copy(at, device):
            return remote(
                hop_out.at[at], right_in.at[at], hop_send.at[layer, at], right_recv.at[layer, at], device
            )

        def body(i, carry):
            @pl.when(i < steps)
            def _():
                slot = i % 2

                @pl.when(i + 1 < steps)
                def _():
                    for copy in fetch(i + 1, (i + 1) % 2):
                        copy.start()

                for copy in fetch(i, slot):
                    copy.wait()
                part, dest = place(i)
                at = part * chips + dest
                store(sib_out.at[at], product(slot, 1))
                sib_copy(at).start()
                store(own.at[slot], product(slot, 0))

            @pl.when(i >= 1)
            def _():
                j = i - 1
                part, dest = place(j)
                at = part * chips + dest
                sib_copy(at).wait_recv()
                tot[...] = own[j % 2] + sib_in[at].astype(F32)

                @pl.when((dest >= chip) & has_left)
                def _():
                    right_copy(at, sibling).wait_recv()
                    tot[...] += left_in[at].astype(F32)

                @pl.when((dest <= chip) & has_right)
                def _():
                    left_copy(at, sibling).wait_recv()
                    tot[...] += right_in[at].astype(F32)

                @pl.when(dest > chip)
                def _():
                    hop_out[at] = tot[...].astype(BF16)
                    right_copy(at, right).start()

                @pl.when(dest < chip)
                def _():
                    hop_out[at] = tot[...].astype(BF16)
                    left_copy(at, left).start()

                @pl.when(dest == chip)
                def _():
                    finish(part)

            return carry

        lax.fori_loop(0, steps + 1, body, 0)

        def drain():
            def one(i, carry):
                part, dest = place(i)
                at = part * chips + dest
                sib_copy(at).wait_send()

                @pl.when(dest != chip)
                def _():
                    right_copy(at, sibling).wait_send()

                return carry

            lax.fori_loop(0, steps, one, 0)

        return drain

    def finish1(part):
        for b in range(sub_blocks):
            rows = pl.ds(pl.multiple_of(part * sub + b * blk, blk), blk)
            scale = lax.rsqrt(1.0 + to_col(tot1[sub + b : sub + b + 1, :]))
            scale_ref[rows, :] = jnp.broadcast_to(scale, (blk, blk))
            mean = tot1[b * blk : (b + 1) * blk, :] * scale
            high = mean.astype(BF16)
            low = (mean - high.astype(F32)).astype(BF16)
            before = jnp.dot(high, w1_ref[:, :hid], preferred_element_type=F32)
            before += jnp.dot(low, w1_ref[:, :hid], preferred_element_type=F32)
            before += jnp.dot(x_ref[rows, :], w1_ref[:, hid:], preferred_element_type=F32)
            hidden = jnp.tanh(before).astype(BF16)
            h1_ref[rows, :] = hidden
            panel2[my_row, rows, :] = jnp.dot(
                hidden, w2_ref[:, :hid], preferred_element_type=F32
            ).astype(BF16)
        share(1, part2, part)

    drain1 = aggregate(
        0, panel1, own1, tot1, sib_out1, sib_in1, hop_out1, left_in1, right_in1, finish1
    )
    for copy in fetch(0, 0):
        copy.start()
    gathered(1, part2, False)

    def finish2(part):
        for b in range(sub_blocks):
            rows = pl.ds(pl.multiple_of(part * sub + b * blk, blk), blk)
            before = jnp.dot(h1_ref[rows, :], w2_ref[:, hid:], preferred_element_type=F32)
            before += tot2[b * blk : (b + 1) * blk, :] * scale_ref[rows, 0:1] + b2_ref[...]
            panel3[my_row * dev_blocks + part * sub_blocks + b] = jnp.tanh(before).astype(BF16)
        share(2, part3, part)

    drain2 = aggregate(
        1, panel2, own2, tot2, sib_out2, sib_in2, hop_out2, left_in2, right_in2, finish2
    )

    def attr_block(b, carry):
        rows = pl.ds(pl.multiple_of(b * blk, blk), blk)
        rebuilt = jnp.dot(
            panel3[my_row * dev_blocks + b], wa_ref[...], preferred_element_type=F32
        )
        diff = rebuilt + ba_ref[...] - x_ref[rows, :].astype(F32)
        error = jnp.sqrt(jnp.mean(diff * diff, axis=1, keepdims=True) + epsilon)
        attr_ref[rows, :] = jnp.broadcast_to(error, (blk, blk))
        return carry

    lax.fori_loop(0, dev_blocks, attr_block, 0)
    drain1()
    drain2()
    for stage, view in enumerate((part1, part2, part3)):
        gathered(stage, view, True)
    gathered(2, part3, False)

    pair_count = pair_ref.shape[1]

    def decode(b, carry):
        rows = pl.ds(pl.multiple_of(b * blk, blk), blk)
        mine = panel3[my_row * dev_blocks + b]
        total = jnp.zeros((blk, blk), F32)
        for j in range(pair_count):
            logits = lax.dot_general(
                mine,
                panel3[pair_ref[b, j]],
                (((1,), (1,)), ((), ())),
                preferred_element_type=F32,
            ) * hid ** (-0.5)
            diff = jax.nn.sigmoid(logits) - target_ref[rows, j * blk : (j + 1) * blk].astype(F32)
            total += diff * diff
        mean = jnp.sum(total, axis=1, keepdims=True) * (1.0 / (pair_count * blk))
        score = mix_alpha * attr_ref[rows, :] + (1.0 - mix_alpha) * jnp.sqrt(mean + epsilon)
        out_ref[pl.ds(b, 1), :] = to_row(score)
        return carry

    lax.fori_loop(0, dev_blocks, decode, 0)


def per_device(
    attributes,
    adj_values,
    adj_rows,
    adj_cols,
    adj_count,
    pair_ids,
    struct_target,
    w_first,
    w_rest,
    layer_bias,
    w_attr,
    attr_bias,
):
    n_row = lax.axis_size("row")
    n_col = lax.axis_size("col")
    nodes, f_in = attributes.shape
    blk = adj_values.shape[3]
    hid = w_rest.shape[1]
    row_blocks = n_col * nodes // blk
    col_blocks = n_row * nodes // blk
    dense = dense_tile(
        adj_values[0, 0], adj_rows[0, 0], adj_cols[0, 0], adj_count[0], row_blocks, col_blocks
    )
    sub = nodes // SUBS
    steps = SUBS * (n_col // 2)
    wide = 2 * blk
    vmem = pl.BlockSpec(memory_space=pltpu.VMEM)
    ring1 = pltpu.VMEM((steps, sub + DEG_ROWS, f_in), BF16)
    ring2 = pltpu.VMEM((steps, sub, hid), BF16)
    scores = pl.pallas_call(
        functools.partial(graph_kernel, n_row, n_col),
        out_shape=jax.ShapeDtypeStruct((nodes // blk, blk), F32),
        in_specs=[
            vmem,
            pl.BlockSpec(memory_space=pl.ANY),
            pl.BlockSpec(memory_space=pltpu.SMEM),
        ]
        + [vmem] * 6,
        out_specs=vmem,
        scratch_shapes=[
            pltpu.VMEM((n_row, nodes, f_in + blk), BF16),
            pltpu.VMEM((n_row, nodes, hid), BF16),
            pltpu.VMEM((col_blocks, blk, hid), BF16),
            pltpu.VMEM((2, 2, sub, col_blocks * blk), BF16),
            pltpu.VMEM((2, sub + DEG_ROWS, f_in), F32),
            pltpu.VMEM((2, sub, hid), F32),
            pltpu.VMEM((sub + DEG_ROWS, f_in), F32),
            pltpu.VMEM((sub, hid), F32),
            pltpu.VMEM((nodes, hid), BF16),
            pltpu.VMEM((nodes, blk), F32),
            pltpu.VMEM((nodes, blk), F32),
        ]
        + [ring1] * 5
        + [ring2] * 5
        + [
            pltpu.SemaphoreType.DMA((2, 2)),
            pltpu.SemaphoreType.DMA((3, n_row - 1, SUBS)),
            pltpu.SemaphoreType.DMA((3, n_row - 1, SUBS)),
            pltpu.SemaphoreType.DMA((2, steps)),
            pltpu.SemaphoreType.DMA((2, steps)),
            pltpu.SemaphoreType.DMA((2, steps)),
            pltpu.SemaphoreType.DMA((2, steps)),
            pltpu.SemaphoreType.DMA((2, steps)),
        ],
        compiler_params=pltpu.CompilerParams(
            collective_id=0, has_side_effects=True, vmem_limit_bytes=56 * 1024 * 1024
        ),
        name="graph_layers",
    )(
        attributes,
        dense,
        pair_ids,
        struct_target.reshape(nodes, -1),
        w_first,
        w_rest[0],
        layer_bias,
        w_attr,
        attr_bias.reshape(1, -1),
    )
    return scores.reshape(nodes)


def solution(mesh):
    return jax.shard_map(
        per_device,
        mesh=mesh,
        in_specs=(
            P(("row", "col"), None),
            P("row", "col", None, None, None),
            P("row", "col", None),
            P("row", "col", None),
            P("row", "col"),
            P(("row", "col"), None),
            P(("row", "col"), None, None),
            P(),
            P(),
            P(),
            P(),
            P(),
        ),
        out_specs=P(("row", "col")),
        check_vma=False,
    )
```

time: 377 us -> 112 us (0.30)
  waiting for transfers between devices: 190 us -> 0 us
  Pallas kernels: 0 us -> 105 us
  blocking collectives: 75.8 us -> 0 us
  other arithmetic: 59.3 us -> 0 us
  matrix products: 21.2 us -> 0 us
  between operations: 14.7 us -> 0.66 us
  local copies, waits for them, and re-layouts: 14 us -> 4.52 us
    reduce_scatter x2 -> x0, waiting for transfers between devices: 112 us -> none  [per_device(): lax.psum_scatter(flattened.astype(jnp.bfloat16), 'col', scatter_dimension...]
    pallas_call x0 -> x2, Pallas kernels: none -> 105 us  [the longest x1 95.3 us: per_device(): pl.pallas_call(functools.partial(graph_kernel, n_row, n_col), out_shape=j...]
    all_gather x3 -> x0, waiting for transfers between devices: 78.2 us -> none  [column_panel(): gathered = lax.all_gather(features, 'row', axis=0, tiled=True)]
    unnamed x1 -> x0, blocking collectives: 75.8 us -> none
    scatter-add x5 -> x0, other arithmetic: 41.1 us -> none  [the longest x4 39.8 us: add_group(): return carried.at[rows_now].add(products * live_mask[:, None, None])]
    dot_general x8 -> x0, matrix products: 21.2 us -> none  [the longest x4 15.8 us: add_group(): jnp.einsum('gij,gjf->gif', vals_now, picked, preferred_element_type=jnp.f...]
    convert_element_type x5 -> x0, other arithmetic: 9.6 us -> none  [the longest x2 7.76 us: per_device(): flattened.astype(jnp.bfloat16)]
    another operation x2 -> x0, local copies, waits for them, and re-layouts: 4.94 us -> none
  transfers between devices with their start and end apart: 5 -> 0, of which waited for: 5 -> 0; matrix products, arithmetic and copies ran while one was open for 2% -> 0% of each run, Pallas kernels for 0% -> 0%
where the time goes in v1:
time: 112 us; the launch traced here: 111 us
  Pallas kernels  105 us (94%)
  local copies, waits for them, and re-layouts  4.52 us (4%)
    pallas_call x1, Pallas kernels, per_device(): pl.pallas_call(functools.partial(graph_kernel, n_row, n_col), out_shape=j...  95.3 us
    pallas_call x1, Pallas kernels, dense_tile(): pl.pallas_call(functools.partial(dense_kernel, part_blocks), grid_spec=gr...  10.1 us
    unnamed x6, local copies, waits for them, and re-layouts  4.52 us

profile of v1, /device:TPU:0, one launch (start us, length us, event | category | flops | bytes accessed | tf_op | source)
XLA Modules:
  0.0 110.6 jit_solution(16122322257375593442)
XLA Ops:
  0.7 1.9 %copy.15 = bf16[64,8,4,128]{3,1,2,0:T(8,128)(2,1)} copy(bf16[64,8,4,128]{3,2,1,0:T(4,128)(2,1)} %bitcast.16) | data formatting | bytes 1048576
  2.6 0.0 copy-start
  2.6 0.7 copy-done
  3.2 0.0 copy-start.1
  3.2 0.7 copy-done.1
  3.9 10.1 %dense_tile.1.a_ref = bf16[4096,2048]{1,0:T(8,128)(2,1)} custom-call(s32[192]{0:T(256)S(1)} %bitcast.12, s32[192]{0:T(256)S(1)} %bitcast.13, s32[1]{0:T(128)} %bitcast.11.count_ref, bf16[192,128,128]{2,1,0:T(8,128)(2,1)} %bitcast.14), custom_call_target="tpu_custom_call" | custom-call | tf_op jit(solution)/shard_map/dense_tile/pallas_call | solution.py:49
  14.0 95.3 %graph_layers.1 = f32[4,128]{1,0:T(4,128)} custom-call(bf16[512,128]{1,0:T(8,128)(2,1)} %x_ref.1, bf16[4096,2048]{1,0:T(8,128)(2,1)} %dense_tile.1.a_ref, s32[4,4]{1,0:T(4,128)} %pair_ref.1, bf16[512,512]{1,0:T(8,128)(2,1)} %bitcast.15, bf16[128,512]{1,0:T(8,128)(2,1)} %w1_ref.1, bf16[256,512]{1,0:T(8,128)(2,1)} %bitcast.17, f32[1,256]{1,0:T(1,128)} %b2_ref.1, ...), custom_call_target="tpu_custom_call" | custom-call | tf_op jit(solution)/shard_map/graph_layers/pallas_call | solution.py:441
  109.3 1.3 %copy.18 = f32[512]{0:T(512)} copy(f32[512]{0:T(512)} %bitcast.18) | data formatting | bytes 4096
Async XLA Ops:
  2.6 0.7 copy-start
  3.2 0.7 copy-start.1

commit v2 on v1

--- a/solution.py
+++ b/solution.py
@@ -12,45 +12,73 @@
 MESH = pl.DeviceIdType.MESH
 F32 = jnp.float32
 BF16 = jnp.bfloat16
-SUBS = 2
+SUBS = 4
+LAG = 2
 DEG_ROWS = 16
 
 
-def dense_kernel(part_blocks, rows_ref, cols_ref, count_ref, vals_ref, out_ref):
+def dense_kernel(part_blocks, rows_ref, cols_ref, count_ref, vals_hbm, out_ref, vals_ref, lists, sizes, sem):
     part = pl.program_id(0)
     blk = vals_ref.shape[1]
+    load = pltpu.make_async_copy(vals_hbm, vals_ref, sem)
+
+    @pl.when(part == 0)
+    def _():
+        load.start()
+        for q in range(sizes.shape[0]):
+            sizes[q] = 0
+
+        def assign(k, carry):
+            q = lax.div(rows_ref[k], part_blocks)
+            n = sizes[q]
+            lists[q, n] = k
+            sizes[q] = n + 1
+            return carry
+
+        lax.fori_loop(0, count_ref[0], assign, 0)
+
     out_ref[...] = jnp.zeros_like(out_ref)
 
-    def add_slot(k, carry):
+    @pl.when(part == 0)
+    def _():
+        load.wait()
+
+    def add_slot(n, carry):
+        k = lists[part, n]
         row = rows_ref[k] - part * part_blocks
-
-        @pl.when((row >= 0) & (row < part_blocks))
-        def _():
-            where_r = pl.ds(pl.multiple_of(row * blk, blk), blk)
-            where_c = pl.ds(pl.multiple_of(cols_ref[k] * blk, blk), blk)
-            out_ref[where_r, where_c] = out_ref[where_r, where_c] + vals_ref[k]
-
+        where_r = pl.ds(pl.multiple_of(row * blk, blk), blk)
+        where_c = pl.ds(pl.multiple_of(cols_ref[k] * blk, blk), blk)
+        out_ref[where_r, where_c] = out_ref[where_r, where_c] + vals_ref[k]
         return carry
 
-    lax.fori_loop(0, count_ref[0], add_slot, 0)
+    lax.fori_loop(0, sizes[part], add_slot, 0)
 
 
 def dense_tile(vals, row_ids, col_ids, count, row_blocks, col_blocks):
     cap, blk, _ = vals.shape
-    part_blocks = 8
+    part_blocks = 4
+    parts = row_blocks // part_blocks
     grid_spec = pltpu.PrefetchScalarGridSpec(
         num_scalar_prefetch=3,
-        grid=(row_blocks // part_blocks,),
-        in_specs=[
-            pl.BlockSpec((cap, blk, blk), lambda i, *_: (0, 0, 0), pipeline_mode=pl.Buffered(1))
+        grid=(parts,),
+        in_specs=[pl.BlockSpec(memory_space=pl.ANY)],
+        out_specs=pl.BlockSpec((part_blocks * blk, col_blocks * blk), lambda i, *_: (i, 0)),
+        scratch_shapes=[
+            pltpu.VMEM((cap, blk, blk), vals.dtype),
+            pltpu.SMEM((parts, cap), jnp.int32),
+            pltpu.SMEM((parts,), jnp.int32),
+            pltpu.SemaphoreType.DMA,
         ],
-        out_specs=pl.BlockSpec((part_blocks * blk, col_blocks * blk), lambda i, *_: (i, 0)),
-    )
+    )
+    dense_bytes = row_blocks * col_blocks * blk * blk * 2
     return pl.pallas_call(
         functools.partial(dense_kernel, part_blocks),
         grid_spec=grid_spec,
         out_shape=jax.ShapeDtypeStruct((row_blocks * blk, col_blocks * blk), vals.dtype),
         compiler_params=pltpu.CompilerParams(vmem_limit_bytes=48 * 1024 * 1024),
+        cost_estimate=pl.CostEstimate(
+            flops=dense_bytes, bytes_accessed=2 * dense_bytes, transcendentals=0
+        ),
         name="dense_tile",
     )(row_ids, col_ids, count, vals)
 
@@ -58,7 +86,11 @@
 def graph_kernel(
     n_row,
     n_col,
-    x_ref,
+    *refs,
+):
+    x_refs, refs = refs[:n_row], refs[n_row:]
+    x_ref = x_refs[0]
+    (
     a_ref,
     pair_ref,
     target_ref,
@@ -97,7 +129,7 @@
     hop_send,
     left_recv,
     right_recv,
-):
+    ) = refs
     my_row = lax.axis_index("row")
     my_col = lax.axis_index("col")
     chips = n_col // 2
@@ -123,6 +155,10 @@
     toward = jnp.where(2 * chip < chips - 1, 1, -1)
 
     def place(i):
+        r = i % chips
+        later = (r == chips - 1) & (i < steps - 1)
+        earlier = (r == 0) & (i > 0)
+        i = i + jnp.where(later, 1, 0) - jnp.where(earlier, 1, 0)
         part = i // chips
         s = i - part * chips
         s2 = s - (far - near)
@@ -148,7 +184,9 @@
             start = pl.multiple_of((dest * 2 + pick) * nodes + part * sub, sub)
             copies.append(
                 pltpu.make_async_copy(
-                    a_ref.at[pl.ds(start, sub), :], abuf.at[slot, which], a_sem.at[slot, which]
+                    a_ref.at[pl.ds(start, sub), :],
+                    abuf.at[slot, pl.ds(which * sub, sub), :],
+                    a_sem.at[slot, which],
                 )
             )
         return copies
@@ -178,16 +216,15 @@
     def _():
         pl.semaphore_signal(barrier, inc=1, device_id=right, device_id_type=MESH)
 
-    panel1[:, :, f_in:] = jnp.ones((n_row, nodes, panel1.shape[2] - f_in), BF16)
-    panel1[my_row, :, :f_in] = x_ref[...]
+    panel1[:, f_in:] = jnp.ones((n_row * nodes, panel1.shape[1] - f_in), BF16)
+    for d in range(n_row):
+        source = lax.rem(my_row + n_row - d, n_row)
+        panel1[pl.ds(pl.multiple_of(source * nodes, nodes), nodes), :f_in] = x_refs[d][...]
 
     pl.semaphore_wait(barrier, n_row + jnp.minimum(chip, 1) + jnp.minimum(chips - 1 - chip, 1))
 
-    def part1(row, part):
-        return panel1.at[row, pl.ds(part * sub, sub), pl.ds(0, f_in)]
-
     def part2(row, part):
-        return panel2.at[row, pl.ds(part * sub, sub), :]
+        return panel2.at[pl.ds(pl.multiple_of(row * nodes + part * sub, sub), sub), :]
 
     def part3(row, part):
         return panel3.at[pl.ds(row * dev_blocks + part * sub_blocks, sub_blocks)]
@@ -218,22 +255,7 @@
                 else:
                     copy.wait_recv()
 
-    for part in range(SUBS):
-        share(0, part1, part)
-    gathered(0, part1, False)
-
     def aggregate(layer, panel, own, tot, sib_out, sib_in, hop_out, left_in, right_in, finish):
-        def product(slot, which):
-            total = None
-            for r in range(n_row):
-                term = jnp.dot(
-                    abuf[slot, which, :, r * nodes : (r + 1) * nodes],
-                    panel[r],
-                    preferred_element_type=F32,
-                )
-                total = term if total is None else total + term
-            return total
-
         def store(dst, value):
             if layer == 1:
                 dst[...] = value.astype(dst.dtype)
@@ -275,17 +297,18 @@
                     copy.wait()
                 part, dest = place(i)
                 at = part * chips + dest
-                store(sib_out.at[at], product(slot, 1))
+                total = jnp.dot(abuf[slot], panel[...], preferred_element_type=F32)
+                store(sib_out.at[at], total[sub:])
                 sib_copy(at).start()
-                store(own.at[slot], product(slot, 0))
-
-            @pl.when(i >= 1)
+                store(own.at[i % (LAG + 1)], total[:sub])
+
+            @pl.when(i >= LAG)
             def _():
-                j = i - 1
+                j = i - LAG
                 part, dest = place(j)
                 at = part * chips + dest
                 sib_copy(at).wait_recv()
-                tot[...] = own[j % 2] + sib_in[at].astype(F32)
+                tot[...] = own[j % (LAG + 1)] + sib_in[at].astype(F32)
 
                 @pl.when((dest >= chip) & has_left)
                 def _():
@@ -313,7 +336,7 @@
 
             return carry
 
-        lax.fori_loop(0, steps + 1, body, 0)
+        lax.fori_loop(0, steps + LAG, body, 0)
 
         def drain():
             def one(i, carry):
@@ -344,17 +367,18 @@
             before += jnp.dot(x_ref[rows, :], w1_ref[:, hid:], preferred_element_type=F32)
             hidden = jnp.tanh(before).astype(BF16)
             h1_ref[rows, :] = hidden
-            panel2[my_row, rows, :] = jnp.dot(
+            mine = pl.ds(pl.multiple_of(my_row * nodes + part * sub + b * blk, blk), blk)
+            panel2[mine, :] = jnp.dot(
                 hidden, w2_ref[:, :hid], preferred_element_type=F32
             ).astype(BF16)
-        share(1, part2, part)
+        share(0, part2, part)
 
     drain1 = aggregate(
         0, panel1, own1, tot1, sib_out1, sib_in1, hop_out1, left_in1, right_in1, finish1
     )
     for copy in fetch(0, 0):
         copy.start()
-    gathered(1, part2, False)
+    gathered(0, part2, False)
 
     def finish2(part):
         for b in range(sub_blocks):
@@ -362,7 +386,7 @@
             before = jnp.dot(h1_ref[rows, :], w2_ref[:, hid:], preferred_element_type=F32)
             before += tot2[b * blk : (b + 1) * blk, :] * scale_ref[rows, 0:1] + b2_ref[...]
             panel3[my_row * dev_blocks + part * sub_blocks + b] = jnp.tanh(before).astype(BF16)
-        share(2, part3, part)
+        share(1, part3, part)
 
     drain2 = aggregate(
         1, panel2, own2, tot2, sib_out2, sib_in2, hop_out2, left_in2, right_in2, finish2
@@ -381,9 +405,9 @@
     lax.fori_loop(0, dev_blocks, attr_block, 0)
     drain1()
     drain2()
-    for stage, view in enumerate((part1, part2, part3)):
+    for stage, view in enumerate((part2, part3)):
         gathered(stage, view, True)
-    gathered(2, part3, False)
+    gathered(1, part3, False)
 
     pair_count = pair_ref.shape[1]
 
@@ -398,7 +422,7 @@
                 (((1,), (1,)), ((), ())),
                 preferred_element_type=F32,
             ) * hid ** (-0.5)
-            diff = jax.nn.sigmoid(logits) - target_ref[rows, j * blk : (j + 1) * blk].astype(F32)
+            diff = jax.nn.sigmoid(logits) - target_ref[rows, j, :].astype(F32)
             total += diff * diff
         mean = jnp.sum(total, axis=1, keepdims=True) * (1.0 / (pair_count * blk))
         score = mix_alpha * attr_ref[rows, :] + (1.0 - mix_alpha) * jnp.sqrt(mean + epsilon)
@@ -429,6 +453,10 @@
     hid = w_rest.shape[1]
     row_blocks = n_col * nodes // blk
     col_blocks = n_row * nodes // blk
+    others = [
+        lax.ppermute(attributes, "row", [(r, (r + d) % n_row) for r in range(n_row)])
+        for d in range(1, n_row)
+    ]
     dense = dense_tile(
         adj_values[0, 0], adj_rows[0, 0], adj_cols[0, 0], adj_count[0], row_blocks, col_blocks
     )
@@ -441,20 +469,20 @@
     scores = pl.pallas_call(
         functools.partial(graph_kernel, n_row, n_col),
         out_shape=jax.ShapeDtypeStruct((nodes // blk, blk), F32),
-        in_specs=[
-            vmem,
+        in_specs=[vmem] * n_row
+        + [
             pl.BlockSpec(memory_space=pl.ANY),
             pl.BlockSpec(memory_space=pltpu.SMEM),
         ]
         + [vmem] * 6,
         out_specs=vmem,
         scratch_shapes=[
-            pltpu.VMEM((n_row, nodes, f_in + blk), BF16),
-            pltpu.VMEM((n_row, nodes, hid), BF16),
+            pltpu.VMEM((n_row * nodes, f_in + blk), BF16),
+            pltpu.VMEM((n_row * nodes, hid), BF16),
             pltpu.VMEM((col_blocks, blk, hid), BF16),
-            pltpu.VMEM((2, 2, sub, col_blocks * blk), BF16),
-            pltpu.VMEM((2, sub + DEG_ROWS, f_in), F32),
-            pltpu.VMEM((2, sub, hid), F32),
+            pltpu.VMEM((2, 2 * sub, col_blocks * blk), BF16),
+            pltpu.VMEM((LAG + 1, sub + DEG_ROWS, f_in), F32),
+            pltpu.VMEM((LAG + 1, sub, hid), F32),
             pltpu.VMEM((sub + DEG_ROWS, f_in), F32),
             pltpu.VMEM((sub, hid), F32),
             pltpu.VMEM((nodes, hid), BF16),
@@ -465,8 +493,8 @@
         + [ring2] * 5
         + [
             pltpu.SemaphoreType.DMA((2, 2)),
-            pltpu.SemaphoreType.DMA((3, n_row - 1, SUBS)),
-            pltpu.SemaphoreType.DMA((3, n_row - 1, SUBS)),
+            pltpu.SemaphoreType.DMA((2, n_row - 1, SUBS)),
+            pltpu.SemaphoreType.DMA((2, n_row - 1, SUBS)),
             pltpu.SemaphoreType.DMA((2, steps)),
             pltpu.SemaphoreType.DMA((2, steps)),
             pltpu.SemaphoreType.DMA((2, steps)),
@@ -479,9 +507,10 @@
         name="graph_layers",
     )(
         attributes,
+        *others,
         dense,
         pair_ids,
-        struct_target.reshape(nodes, -1),
+        struct_target,
         w_first,
         w_rest[0],
         layer_bias,

time: 112 us -> 109 us (0.973)
  Pallas kernels: 105 us -> 98.2 us
  starting transfers between devices: 0 us -> 5.89 us
  local copies, waits for them, and re-layouts: 4.52 us -> 3.3 us
    pallas_call x1, Pallas kernels: 95.3 us -> 85.5 us  [per_device(): pl.pallas_call(functools.partial(graph_kernel, n_row, n_col), out_shape=j...]
    ppermute x0 -> x3, starting transfers between devices: none -> 5.89 us  [per_device(): lax.ppermute(attributes, 'row', [(r, (r + d) % n_row) for r in range(n_ro...]
    pallas_call x1, Pallas kernels: 10.1 us -> 12.7 us  [dense_tile(): pl.pallas_call(functools.partial(dense_kernel, part_blocks), grid_spec=gr...]
    unnamed x6 -> x11, local copies, waits for them, and re-layouts: 4.52 us -> 3.3 us
  transfers between devices with their start and end apart: 0 -> 3, of which waited for: 0 -> 0; matrix products, arithmetic and copies ran while one was open for 0% -> 0% of each run, Pallas kernels for 0% -> 12%
where the time goes in v2:
time: 109 us; the launch traced here: 108 us
  Pallas kernels  98.2 us (90%)
  starting transfers between devices  5.89 us (5%)
  local copies, waits for them, and re-layouts  3.3 us (3%)
    pallas_call x1, Pallas kernels, per_device(): pl.pallas_call(functools.partial(graph_kernel, n_row, n_col), out_shape=j...  85.5 us
    pallas_call x1, Pallas kernels, dense_tile(): pl.pallas_call(functools.partial(dense_kernel, part_blocks), grid_spec=gr...  12.7 us
    ppermute x3, starting transfers between devices, per_device(): lax.ppermute(attributes, 'row', [(r, (r + d) % n_row) for r in range(n_ro...  5.89 us
    unnamed x11, local copies, waits for them, and re-layouts  3.3 us
  transfers between devices with their start and end apart: 3, of which 0 were waited for; matrix products, arithmetic and copies ran while one was open for 0% of the time, Pallas kernels for 12%

profile of v2, /device:TPU:0, one launch (start us, length us, event | category | flops | bytes accessed | tf_op | source)
XLA Modules:
  0.0 108.1 jit_solution(16930663375330675362)
XLA Ops:
  0.0 3.0 %collective-permute-start.1 = (bf16[512,128]{1,0:T(8,128)(2,1)}, bf16[512,128]{1,0:T(8,128)(2,1)S(1)}, u32[]{:S(2)}, u32[]{:S(2)}) collective-permute-start(bf16[512,128]{1,0:T(8,128)(2,1)} %refs_0_.1), channel_id=1, source_target_pairs={{0,16},{8,24},{16,0},{24,8},{1,17},{9,25},{17,1},{25,9},{2,18},{10... | collective-permute-start | bytes 393224 | tf_op jit(solution)/shard_map/ppermute | solution.py:457
  3.0 1.5 %collective-permute-start = (bf16[512,128]{1,0:T(8,128)(2,1)}, bf16[512,128]{1,0:T(8,128)(2,1)S(1)}, u32[]{:S(2)}, u32[]{:S(2)}) collective-permute-start(bf16[512,128]{1,0:T(8,128)(2,1)} %refs_0_.1), channel_id=1, source_target_pairs={{0,8},{8,16},{16,24},{24,0},{1,9},{9,17},{17,25},{25,1},{2,10},{10... | collective-permute-start | bytes 393224 | tf_op jit(solution)/shard_map/ppermute | solution.py:457
  4.5 1.4 %collective-permute-start.2 = (bf16[512,128]{1,0:T(8,128)(2,1)}, bf16[512,128]{1,0:T(8,128)(2,1)S(1)}, u32[]{:S(2)}, u32[]{:S(2)}) collective-permute-start(bf16[512,128]{1,0:T(8,128)(2,1)} %refs_0_.1), channel_id=1, source_target_pairs={{0,24},{8,0},{16,8},{24,16},{1,25},{9,1},{17,9},{25,17},{2,26},{10... | collective-permute-start | bytes 393224 | tf_op jit(solution)/shard_map/ppermute | solution.py:457
  6.5 0.0 copy-start
  6.6 0.7 copy-done
  7.2 0.0 copy-start.1
  7.2 0.7 copy-done.1
  7.9 12.7 %dense_tile.1.refs_4_ = bf16[4096,2048]{1,0:T(8,128)(2,1)} custom-call(s32[192]{0:T(256)S(1)} %bitcast.8, s32[192]{0:T(256)S(1)} %bitcast.9, s32[1]{0:T(128)} %bitcast.7.count_ref, bf16[192,128,128]{2,1,0:T(8,128)(2,1)} %bitcast.10), custom_call_target="tpu_custom_call" | custom-call | flops 16777216 | bytes 33554432 | tf_op jit(solution)/shard_map/dense_tile/pallas_call | solution.py:74
  20.6 0.0 collective-permute-done.1.refs_2_
  20.6 0.0 copy-start.2
  20.7 0.0 collective-permute-done.refs_1_
  20.7 0.0 copy-start.3
  20.7 0.0 collective-permute-done.2.refs_3_
  20.7 0.0 copy-start.4
  20.7 0.6 copy-done.2
  21.3 0.0 copy-done.3
  21.4 0.0 copy-done.4
  21.4 85.5 %graph_layers.1 = f32[4,128]{1,0:T(4,128)} custom-call(bf16[512,128]{1,0:T(8,128)(2,1)} %refs_0_.1, bf16[512,128]{1,0:T(8,128)(2,1)} %copy-done.3, bf16[512,128]{1,0:T(8,128)(2,1)} %copy-done.2, bf16[512,128]{1,0:T(8,128)(2,1)} %copy-done.4, bf16[4096,2048]{1,0:T(8,128)(2,1)} %dense_tile.1.refs_4_, s32[4,4]{1,0:T(4,128)} %refs_5_.1, ...), custom_call_target="tpu_custom_call" | custom-call | tf_op jit(solution)/shard_map/graph_layers/pallas_call | solution.py:469
  106.9 1.3 %copy.15 = f32[512]{0:T(512)} copy(f32[512]{0:T(512)} %bitcast.12) | data formatting | bytes 4096
Async XLA Ops:
  0.0 20.6 %collective-permute-start.1 = (bf16[512,128]{1,0:T(8,128)(2,1)}, bf16[512,128]{1,0:T(8,128)(2,1)S(1)}, u32[]{:S(2)}, u32[]{:S(2)}) collective-permute-start(bf16[512,128]{1,0:T(8,128)(2,1)} %refs_0_.1), channel_id=1, source_target_pairs={{0,16},{8,24},{16,0},{24,8},{1,17},{9,25},{17,1},{25,9},{2,18},{10... | collective-permute-start | bytes 393224 | tf_op jit(solution)/shard_map/ppermute | solution.py:457
  3.0 17.7 %collective-permute-start = (bf16[512,128]{1,0:T(8,128)(2,1)}, bf16[512,128]{1,0:T(8,128)(2,1)S(1)}, u32[]{:S(2)}, u32[]{:S(2)}) collective-permute-start(bf16[512,128]{1,0:T(8,128)(2,1)} %refs_0_.1), channel_id=1, source_target_pairs={{0,8},{8,16},{16,24},{24,0},{1,9},{9,17},{17,25},{25,1},{2,10},{10... | collective-permute-start | bytes 393224 | tf_op jit(solution)/shard_map/ppermute | solution.py:457
  4.5 16.2 %collective-permute-start.2 = (bf16[512,128]{1,0:T(8,128)(2,1)}, bf16[512,128]{1,0:T(8,128)(2,1)S(1)}, u32[]{:S(2)}, u32[]{:S(2)}) collective-permute-start(bf16[512,128]{1,0:T(8,128)(2,1)} %refs_0_.1), channel_id=1, source_target_pairs={{0,24},{8,0},{16,8},{24,16},{1,25},{9,1},{17,9},{25,17},{2,26},{10... | collective-permute-start | bytes 393224 | tf_op jit(solution)/shard_map/ppermute | solution.py:457
  6.5 0.7 copy-start
  7.2 0.7 copy-start.1
  20.6 0.7 copy-start.2
  20.7 0.7 copy-start.3
  20.7 0.7 copy-start.4

commit v3 on v2

--- a/solution.py
+++ b/solution.py
@@ -12,8 +12,8 @@
 MESH = pl.DeviceIdType.MESH
 F32 = jnp.float32
 BF16 = jnp.bfloat16
-SUBS = 4
-LAG = 2
+SUBS = 2
+GROUP = 2
 DEG_ROWS = 16
 
 
@@ -29,13 +29,13 @@
             sizes[q] = 0
 
         def assign(k, carry):
-            q = lax.div(rows_ref[k], part_blocks)
+            q = lax.div(rows_ref[0, 0, k], part_blocks)
             n = sizes[q]
             lists[q, n] = k
             sizes[q] = n + 1
             return carry
 
-        lax.fori_loop(0, count_ref[0], assign, 0)
+        lax.fori_loop(0, count_ref[0, 0], assign, 0)
 
     out_ref[...] = jnp.zeros_like(out_ref)
 
@@ -45,9 +45,9 @@
 
     def add_slot(n, carry):
         k = lists[part, n]
-        row = rows_ref[k] - part * part_blocks
+        row = rows_ref[0, 0, k] - part * part_blocks
         where_r = pl.ds(pl.multiple_of(row * blk, blk), blk)
-        where_c = pl.ds(pl.multiple_of(cols_ref[k] * blk, blk), blk)
+        where_c = pl.ds(pl.multiple_of(cols_ref[0, 0, k] * blk, blk), blk)
         out_ref[where_r, where_c] = out_ref[where_r, where_c] + vals_ref[k]
         return carry
 
@@ -58,22 +58,19 @@
     cap, blk, _ = vals.shape
     part_blocks = 4
     parts = row_blocks // part_blocks
-    grid_spec = pltpu.PrefetchScalarGridSpec(
-        num_scalar_prefetch=3,
+    dense_bytes = row_blocks * col_blocks * blk * blk * 2
+    return pl.pallas_call(
+        functools.partial(dense_kernel, part_blocks),
         grid=(parts,),
-        in_specs=[pl.BlockSpec(memory_space=pl.ANY)],
-        out_specs=pl.BlockSpec((part_blocks * blk, col_blocks * blk), lambda i, *_: (i, 0)),
+        in_specs=[pl.BlockSpec(memory_space=pltpu.SMEM)] * 3
+        + [pl.BlockSpec(memory_space=pl.ANY)],
+        out_specs=pl.BlockSpec((part_blocks * blk, col_blocks * blk), lambda i: (i, 0)),
         scratch_shapes=[
             pltpu.VMEM((cap, blk, blk), vals.dtype),
             pltpu.SMEM((parts, cap), jnp.int32),
             pltpu.SMEM((parts,), jnp.int32),
             pltpu.SemaphoreType.DMA,
         ],
-    )
-    dense_bytes = row_blocks * col_blocks * blk * blk * 2
-    return pl.pallas_call(
-        functools.partial(dense_kernel, part_blocks),
-        grid_spec=grid_spec,
         out_shape=jax.ShapeDtypeStruct((row_blocks * blk, col_blocks * blk), vals.dtype),
         compiler_params=pltpu.CompilerParams(vmem_limit_bytes=48 * 1024 * 1024),
         cost_estimate=pl.CostEstimate(
@@ -86,11 +83,7 @@
 def graph_kernel(
     n_row,
     n_col,
-    *refs,
-):
-    x_refs, refs = refs[:n_row], refs[n_row:]
-    x_ref = x_refs[0]
-    (
+    x_ref,
     a_ref,
     pair_ref,
     target_ref,
@@ -129,7 +122,8 @@
     hop_send,
     left_recv,
     right_recv,
-    ) = refs
+    prod,
+):
     my_row = lax.axis_index("row")
     my_col = lax.axis_index("col")
     chips = n_col // 2
@@ -176,19 +170,20 @@
     def to_col(row):
         return jnp.sum(jnp.where(eye, jnp.broadcast_to(row, (blk, blk)), 0.0), axis=1, keepdims=True)
 
-    def fetch(i, slot):
-        part, dest = place(i)
+    def fetch(group, slot):
         copies = []
-        for which in range(2):
-            pick = core if which == 0 else 1 - core
-            start = pl.multiple_of((dest * 2 + pick) * nodes + part * sub, sub)
-            copies.append(
-                pltpu.make_async_copy(
-                    a_ref.at[pl.ds(start, sub), :],
-                    abuf.at[slot, pl.ds(which * sub, sub), :],
-                    a_sem.at[slot, which],
+        for u in range(GROUP):
+            part, dest = place(group * GROUP + u)
+            for which in range(2):
+                pick = core if which == 0 else 1 - core
+                start = pl.multiple_of((dest * 2 + pick) * nodes + part * sub, sub)
+                copies.append(
+                    pltpu.make_async_copy(
+                        a_ref.at[pl.ds(start, sub), :],
+                        abuf.at[slot, pl.ds((which * GROUP + u) * sub, sub), :],
+                        a_sem.at[slot, which * GROUP + u],
+                    )
                 )
-            )
         return copies
 
     def remote(src, dst, send, recv, device):
@@ -217,11 +212,13 @@
         pl.semaphore_signal(barrier, inc=1, device_id=right, device_id_type=MESH)
 
     panel1[:, f_in:] = jnp.ones((n_row * nodes, panel1.shape[1] - f_in), BF16)
-    for d in range(n_row):
-        source = lax.rem(my_row + n_row - d, n_row)
-        panel1[pl.ds(pl.multiple_of(source * nodes, nodes), nodes), :f_in] = x_refs[d][...]
+    panel1[pl.ds(pl.multiple_of(my_row * nodes, nodes), nodes), :f_in] = x_ref[...]
 
     pl.semaphore_wait(barrier, n_row + jnp.minimum(chip, 1) + jnp.minimum(chips - 1 - chip, 1))
+
+    def part1(row, part):
+        rows = pl.ds(pl.multiple_of(row * nodes + part * sub, sub), sub)
+        return panel1.at[rows, pl.ds(0, f_in)]
 
     def part2(row, part):
         return panel2.at[pl.ds(pl.multiple_of(row * nodes + part * sub, sub), sub), :]
@@ -239,26 +236,29 @@
                 peers[d - 1],
             ).start()
 
-    def gathered(stage, view, sent):
+    def arrived_from(stage, view, d):
+        source = lax.rem(my_row + n_row - d, n_row)
         for part in range(SUBS):
-            for d in range(1, n_row):
-                source = lax.rem(my_row + n_row - d, n_row)
-                copy = remote(
-                    view(my_row if sent else source, part),
-                    view(my_row if sent else source, part),
-                    g_send.at[stage, d - 1, part],
-                    g_recv.at[stage, d - 1, part],
-                    peers[d - 1],
-                )
-                if sent:
-                    copy.wait_send()
-                else:
-                    copy.wait_recv()
-
-    def aggregate(layer, panel, own, tot, sib_out, sib_in, hop_out, left_in, right_in, finish):
+            where = view(source, part)
+            remote(
+                where, where, g_send.at[stage, d - 1, part], g_recv.at[stage, d - 1, part], sibling
+            ).wait_recv()
+
+    def shared(stage, view):
+        for d in range(1, n_row):
+            for part in range(SUBS):
+                where = view(my_row, part)
+                remote(
+                    where, where, g_send.at[stage, d - 1, part], g_recv.at[stage, d - 1, part], sibling
+                ).wait_send()
+
+    for part in range(SUBS):
+        share(0, part1, part)
+
+    def aggregate(layer, panel, view, own, tot, sib_out, sib_in, hop_out, left_in, right_in, finish):
         def store(dst, value):
             if layer == 1:
-                dst[...] = value.astype(dst.dtype)
+                dst[...] = value[...].astype(dst.dtype)
                 return
             dst[:sub, :] = value[:, :f_in].astype(dst.dtype)
             lane = lax.broadcasted_iota(jnp.int32, (DEG_ROWS, blk), 0)
@@ -283,60 +283,101 @@
                 hop_out.at[at], right_in.at[at], hop_send.at[layer, at], right_recv.at[layer, at], device
             )
 
-        def body(i, carry):
-            @pl.when(i < steps)
+        groups = steps // GROUP
+
+        def multiply(group, slot):
+            prod[...] = jnp.zeros_like(prod)
+
+            def add_panel(d, carry):
+                @pl.when((group == 0) & (d > 0))
+                def _():
+                    arrived_from(layer, view, d)
+
+                source = lax.rem(my_row + n_row - d, n_row)
+                span = pl.ds(pl.multiple_of(source * nodes, nodes), nodes)
+                prod[...] += jnp.dot(
+                    abuf[slot, :, span], panel[span, :], preferred_element_type=F32
+                )
+                return carry
+
+            lax.fori_loop(0, n_row, add_panel, 0)
+
+        def body(group, carry):
+            @pl.when(group < groups)
             def _():
-                slot = i % 2
-
-                @pl.when(i + 1 < steps)
+                slot = group % 2
+
+                @pl.when(group + 1 < groups)
                 def _():
-                    for copy in fetch(i + 1, (i + 1) % 2):
+                    for copy in fetch(group + 1, (group + 1) % 2):
                         copy.start()
 
-                for copy in fetch(i, slot):
+                for copy in fetch(group, slot):
                     copy.wait()
-                part, dest = place(i)
-                at = part * chips + dest
-                total = jnp.dot(abuf[slot], panel[...], preferred_element_type=F32)
-                store(sib_out.at[at], total[sub:])
-                sib_copy(at).start()
-                store(own.at[i % (LAG + 1)], total[:sub])
-
-            @pl.when(i >= LAG)
-            def _():
-                j = i - LAG
+                multiply(group, slot)
+                for u in range(GROUP):
+                    part, dest = place(group * GROUP + u)
+                    at = part * chips + dest
+                    first = (GROUP + u) * sub
+                    store(sib_out.at[at], prod.at[first : first + sub])
+                    sib_copy(at).start()
+                for u in range(GROUP):
+                    store(own.at[slot * GROUP + u], prod.at[u * sub : (u + 1) * sub])
+
+            def reduce(u, carry):
+                j = (group - 1) * GROUP + u
                 part, dest = place(j)
                 at = part * chips + dest
                 sib_copy(at).wait_recv()
-                tot[...] = own[j % (LAG + 1)] + sib_in[at].astype(F32)
-
-                @pl.when((dest >= chip) & has_left)
-                def _():
-                    right_copy(at, sibling).wait_recv()
-                    tot[...] += left_in[at].astype(F32)
-
-                @pl.when((dest <= chip) & has_right)
-                def _():
-                    left_copy(at, sibling).wait_recv()
-                    tot[...] += right_in[at].astype(F32)
+                mine = own.at[((group - 1) % 2) * GROUP + u]
+
+                def forward(copy, arrived, has_up, device):
+                    @pl.when(has_up)
+                    def _():
+                        copy(at, sibling).wait_recv()
+                        hop_out[at] = (
+                            mine[...] + sib_in[at].astype(F32) + arrived[at].astype(F32)
+                        ).astype(BF16)
+
+                    @pl.when(jnp.logical_not(has_up))
+                    def _():
+                        hop_out[at] = (mine[...] + sib_in[at].astype(F32)).astype(BF16)
+
+                    copy(at, device).start()
 
                 @pl.when(dest > chip)
                 def _():
-                    hop_out[at] = tot[...].astype(BF16)
-                    right_copy(at, right).start()
+                    forward(right_copy, left_in, has_left, right)
 
                 @pl.when(dest < chip)
                 def _():
-                    hop_out[at] = tot[...].astype(BF16)
-                    left_copy(at, left).start()
+                    forward(left_copy, right_in, has_right, left)
 
                 @pl.when(dest == chip)
                 def _():
+                    tot[...] = mine[...] + sib_in[at].astype(F32)
+
+                    @pl.when(has_left)
+                    def _():
+                        right_copy(at, sibling).wait_recv()
+                        tot[...] += left_in[at].astype(F32)
+
+                    @pl.when(has_right)
+                    def _():
+                        left_copy(at, sibling).wait_recv()
+                        tot[...] += right_in[at].astype(F32)
+
                     finish(part)
 
+                return carry
+
+            @pl.when(group >= 1)
+            def _():
+                lax.fori_loop(0, GROUP, reduce, 0)
+
             return carry
 
-        lax.fori_loop(0, steps + LAG, body, 0)
+        lax.fori_loop(0, groups + 1, body, 0)
 
         def drain():
             def one(i, carry):
@@ -371,14 +412,13 @@
             panel2[mine, :] = jnp.dot(
                 hidden, w2_ref[:, :hid], preferred_element_type=F32
             ).astype(BF16)
-        share(0, part2, part)
+        share(1, part2, part)
 
     drain1 = aggregate(
-        0, panel1, own1, tot1, sib_out1, sib_in1, hop_out1, left_in1, right_in1, finish1
+        0, panel1, part1, own1, tot1, sib_out1, sib_in1, hop_out1, left_in1, right_in1, finish1
     )
     for copy in fetch(0, 0):
         copy.start()
-    gathered(0, part2, False)
 
     def finish2(part):
         for b in range(sub_blocks):
@@ -386,10 +426,10 @@
             before = jnp.dot(h1_ref[rows, :], w2_ref[:, hid:], preferred_element_type=F32)
             before += tot2[b * blk : (b + 1) * blk, :] * scale_ref[rows, 0:1] + b2_ref[...]
             panel3[my_row * dev_blocks + part * sub_blocks + b] = jnp.tanh(before).astype(BF16)
-        share(1, part3, part)
+        share(2, part3, part)
 
     drain2 = aggregate(
-        1, panel2, own2, tot2, sib_out2, sib_in2, hop_out2, left_in2, right_in2, finish2
+        1, panel2, part2, own2, tot2, sib_out2, sib_in2, hop_out2, left_in2, right_in2, finish2
     )
 
     def attr_block(b, carry):
@@ -405,9 +445,10 @@
     lax.fori_loop(0, dev_blocks, attr_block, 0)
     drain1()
     drain2()
-    for stage, view in enumerate((part2, part3)):
-        gathered(stage, view, True)
-    gathered(1, part3, False)
+    for stage, view in enumerate((part1, part2, part3)):
+        shared(stage, view)
+    for d in range(1, n_row):
+        arrived_from(2, part3, d)
 
     pair_count = pair_ref.shape[1]
 
@@ -453,12 +494,8 @@
     hid = w_rest.shape[1]
     row_blocks = n_col * nodes // blk
     col_blocks = n_row * nodes // blk
-    others = [
-        lax.ppermute(attributes, "row", [(r, (r + d) % n_row) for r in range(n_row)])
-        for d in range(1, n_row)
-    ]
     dense = dense_tile(
-        adj_values[0, 0], adj_rows[0, 0], adj_cols[0, 0], adj_count[0], row_blocks, col_blocks
+        adj_values[0, 0], adj_rows, adj_cols, adj_count, row_blocks, col_blocks
     )
     sub = nodes // SUBS
     steps = SUBS * (n_col // 2)
@@ -469,8 +506,8 @@
     scores = pl.pallas_call(
         functools.partial(graph_kernel, n_row, n_col),
         out_shape=jax.ShapeDtypeStruct((nodes // blk, blk), F32),
-        in_specs=[vmem] * n_row
-        + [
+        in_specs=[
+            vmem,
             pl.BlockSpec(memory_space=pl.ANY),
             pl.BlockSpec(memory_space=pltpu.SMEM),
         ]
@@ -480,9 +517,9 @@
             pltpu.VMEM((n_row * nodes, f_in + blk), BF16),
             pltpu.VMEM((n_row * nodes, hid), BF16),
             pltpu.VMEM((col_blocks, blk, hid), BF16),
-            pltpu.VMEM((2, 2 * sub, col_blocks * blk), BF16),
-            pltpu.VMEM((LAG + 1, sub + DEG_ROWS, f_in), F32),
-            pltpu.VMEM((LAG + 1, sub, hid), F32),
+            pltpu.VMEM((2, 2 * GROUP * sub, col_blocks * blk), BF16),
+            pltpu.VMEM((2 * GROUP, sub + DEG_ROWS, f_in), F32),
+            pltpu.VMEM((2 * GROUP, sub, hid), F32),
             pltpu.VMEM((sub + DEG_ROWS, f_in), F32),
             pltpu.VMEM((sub, hid), F32),
             pltpu.VMEM((nodes, hid), BF16),
@@ -492,14 +529,15 @@
         + [ring1] * 5
         + [ring2] * 5
         + [
-            pltpu.SemaphoreType.DMA((2, 2)),
-            pltpu.SemaphoreType.DMA((2, n_row - 1, SUBS)),
-            pltpu.SemaphoreType.DMA((2, n_row - 1, SUBS)),
+            pltpu.SemaphoreType.DMA((2, 2 * GROUP)),
+            pltpu.SemaphoreType.DMA((3, n_row - 1, SUBS)),
+            pltpu.SemaphoreType.DMA((3, n_row - 1, SUBS)),
             pltpu.SemaphoreType.DMA((2, steps)),
             pltpu.SemaphoreType.DMA((2, steps)),
             pltpu.SemaphoreType.DMA((2, steps)),
             pltpu.SemaphoreType.DMA((2, steps)),
             pltpu.SemaphoreType.DMA((2, steps)),
+            pltpu.VMEM((2 * GROUP * sub, wide), F32),
         ],
         compiler_params=pltpu.CompilerParams(
             collective_id=0, has_side_effects=True, vmem_limit_bytes=56 * 1024 * 1024
@@ -507,7 +545,6 @@
         name="graph_layers",
     )(
         attributes,
-        *others,
         dense,
         pair_ids,
         struct_target,

time: 109 us -> 92 us (0.84)
  Pallas kernels: 98.2 us -> 87.9 us
  starting transfers between devices: 5.89 us -> 0 us
    pallas_call x1, Pallas kernels: 85.5 us -> 77.8 us  [per_device(): pl.pallas_call(functools.partial(graph_kernel, n_row, n_col), out_shape=j...]
    ppermute x3 -> x0, starting transfers between devices: 5.89 us -> none  [per_device(): lax.ppermute(attributes, 'row', [(r, (r + d) % n_row) for r in range(n_ro...]
    pallas_call x1, Pallas kernels: 12.7 us -> 10.1 us  [dense_tile(): pl.pallas_call(functools.partial(dense_kernel, part_blocks), grid=(parts,...]
    unnamed x11 -> x5, local copies, waits for them, and re-layouts: 3.3 us -> 2.6 us
  transfers between devices with their start and end apart: 3 -> 0, of which waited for: 0 -> 0; matrix products, arithmetic and copies ran while one was open for 0% -> 0% of each run, Pallas kernels for 12% -> 0%
where the time goes in v3:
time: 92 us; the launch traced here: 91.2 us
  Pallas kernels  87.9 us (96%)
  local copies, waits for them, and re-layouts  2.6 us (3%)
    pallas_call x1, Pallas kernels, per_device(): pl.pallas_call(functools.partial(graph_kernel, n_row, n_col), out_shape=j...  77.8 us
    pallas_call x1, Pallas kernels, dense_tile(): pl.pallas_call(functools.partial(dense_kernel, part_blocks), grid=(parts,...  10.1 us
    unnamed x5, local copies, waits for them, and re-layouts  2.6 us

profile of v3, /device:TPU:0, one launch (start us, length us, event | category | flops | bytes accessed | tf_op | source)
XLA Modules:
  0.0 91.2 jit_solution(9649178472189686520)
XLA Ops:
  0.7 0.0 copy-start
  0.7 0.7 copy-done
  1.3 0.0 copy-start.1
  1.3 0.7 copy-done.1
  2.0 10.1 %dense_tile.1.a_ref = bf16[4096,2048]{1,0:T(8,128)(2,1)} custom-call(s32[1,1,192]{2,1,0:T(1,128)S(1)} %copy-done, s32[1,1,192]{2,1,0:T(1,128)S(1)} %copy-done.1, s32[1,1]{1,0:T(1,128)S(6)} %copy.14.count_ref, bf16[192,128,128]{2,1,0:T(8,128)(2,1)} %bitcast.4), custom_call_target="tpu_custom_call" | custom-call | flops 16777216 | bytes 33554432 | tf_op jit(solution)/shard_map/dense_tile/pallas_call | solution.py:62
  12.1 77.8 %graph_layers.1 = f32[4,128]{1,0:T(4,128)} custom-call(bf16[512,128]{1,0:T(8,128)(2,1)} %x_ref.1, bf16[4096,2048]{1,0:T(8,128)(2,1)} %dense_tile.1.a_ref, s32[4,4]{1,0:T(4,128)} %pair_ref.1, bf16[512,4,128]{2,1,0:T(4,128)(2,1)} %target_ref.1, bf16[128,512]{1,0:T(8,128)(2,1)} %w1_ref.1, bf16[256,512]{1,0:T(8,128)(2,1)} %bitcast.5, f32[1,256]{1,0:T(1,128)} %b2_ref.1, ...), custom_call_target="tpu_custom_call" | custom-call | tf_op jit(solution)/shard_map/graph_layers/pallas_call | solution.py:506
  89.9 1.3 %copy.15 = f32[512]{0:T(512)} copy(f32[512]{0:T(512)} %bitcast.6) | data formatting | bytes 4096
Async XLA Ops:
  0.7 0.7 copy-start
  1.3 0.7 copy-start.1

commit v4 on v3

--- a/solution.py
+++ b/solution.py
@@ -13,7 +13,8 @@
 F32 = jnp.float32
 BF16 = jnp.bfloat16
 SUBS = 2
-GROUP = 2
+GROUP = 1
+OWN_LAG = 2
 DEG_ROWS = 16
 
 
@@ -149,12 +150,15 @@
     toward = jnp.where(2 * chip < chips - 1, 1, -1)
 
     def place(i):
-        r = i % chips
-        later = (r == chips - 1) & (i < steps - 1)
-        earlier = (r == 0) & (i > 0)
-        i = i + jnp.where(later, 1, 0) - jnp.where(earlier, 1, 0)
-        part = i // chips
-        s = i - part * chips
+        lag = min(OWN_LAG, chips - 1)
+        first = i < chips - 1
+        j = jnp.maximum(i - (chips - 1), 0)
+        turn = j // chips
+        r = j % chips
+        is_own = jnp.logical_not(first) & ((r == lag) | (i == steps - 1))
+        part = jnp.where(first, 0, jnp.where(is_own, turn, turn + 1))
+        later = jnp.where(is_own, chips - 1, jnp.where(r < lag, r, r - 1))
+        s = jnp.where(first, i, later)
         s2 = s - (far - near)
         paired = chip + (near - s2 // 2) * (1 - 2 * (s2 % 2))
         dest = jnp.where(s < far - near, chip + toward * (far - s), paired)

time: 92 us -> 91.9 us (level)
    pallas_call x1, Pallas kernels: 10.1 us -> 12.9 us  [dense_tile(): pl.pallas_call(functools.partial(dense_kernel, part_blocks), grid=(parts,...]
    pallas_call x1, Pallas kernels: 77.8 us -> 75.4 us  [per_device(): pl.pallas_call(functools.partial(graph_kernel, n_row, n_col), out_shape=j...]
where the time goes in v4:
time: 91.9 us; the launch traced here: 91.6 us
  Pallas kernels  88.3 us (96%)
  local copies, waits for them, and re-layouts  2.6 us (3%)
    pallas_call x1, Pallas kernels, per_device(): pl.pallas_call(functools.partial(graph_kernel, n_row, n_col), out_shape=j...  75.4 us
    pallas_call x1, Pallas kernels, dense_tile(): pl.pallas_call(functools.partial(dense_kernel, part_blocks), grid=(parts,...  12.9 us
    unnamed x5, local copies, waits for them, and re-layouts  2.6 us

profile of v4, /device:TPU:0, one launch (start us, length us, event | category | flops | bytes accessed | tf_op | source)
XLA Modules:
  0.0 91.6 jit_solution(10373587431318800324)
XLA Ops:
  0.7 0.0 copy-start
  0.7 0.7 copy-done
  1.3 0.0 copy-start.1
  1.3 0.7 copy-done.1
  2.0 12.9 %dense_tile.1.a_ref = bf16[4096,2048]{1,0:T(8,128)(2,1)} custom-call(s32[1,1,192]{2,1,0:T(1,128)S(1)} %copy-done, s32[1,1,192]{2,1,0:T(1,128)S(1)} %copy-done.1, s32[1,1]{1,0:T(1,128)S(6)} %copy.14.count_ref, bf16[192,128,128]{2,1,0:T(8,128)(2,1)} %bitcast.4), custom_call_target="tpu_custom_call" | custom-call | flops 16777216 | bytes 33554432 | tf_op jit(solution)/shard_map/dense_tile/pallas_call | solution.py:63
  14.9 75.4 %graph_layers.1 = f32[4,128]{1,0:T(4,128)} custom-call(bf16[512,128]{1,0:T(8,128)(2,1)} %x_ref.1, bf16[4096,2048]{1,0:T(8,128)(2,1)} %dense_tile.1.a_ref, s32[4,4]{1,0:T(4,128)} %pair_ref.1, bf16[512,4,128]{2,1,0:T(4,128)(2,1)} %target_ref.1, bf16[128,512]{1,0:T(8,128)(2,1)} %w1_ref.1, bf16[256,512]{1,0:T(8,128)(2,1)} %bitcast.5, f32[1,256]{1,0:T(1,128)} %b2_ref.1, ...), custom_call_target="tpu_custom_call" | custom-call | tf_op jit(solution)/shard_map/graph_layers/pallas_call | solution.py:510
  90.4 1.3 %copy.15 = f32[512]{0:T(512)} copy(f32[512]{0:T(512)} %bitcast.6) | data formatting | bytes 4096
Async XLA Ops:
  0.7 0.7 copy-start
  1.3 0.7 copy-start.1

commit v5 on v4

--- a/solution.py
+++ b/solution.py
@@ -15,6 +15,7 @@
 SUBS = 2
 GROUP = 1
 OWN_LAG = 2
+SLOTS = 4
 DEG_ROWS = 16
 
 
@@ -200,8 +201,9 @@
             device_id_type=MESH,
         )
 
-    for copy in fetch(0, 0):
-        copy.start()
+    for early in range(min(SLOTS - 1, steps // GROUP)):
+        for copy in fetch(early, early):
+            copy.start()
 
     barrier = pltpu.get_barrier_semaphore()
     for device in [sibling] + peers:
@@ -309,11 +311,12 @@
         def body(group, carry):
             @pl.when(group < groups)
             def _():
-                slot = group % 2
-
-                @pl.when(group + 1 < groups)
+                slot = group % SLOTS
+                ahead = group + SLOTS - 1
+
+                @pl.when(ahead < groups)
                 def _():
-                    for copy in fetch(group + 1, (group + 1) % 2):
+                    for copy in fetch(ahead, ahead % SLOTS):
                         copy.start()
 
                 for copy in fetch(group, slot):
@@ -326,7 +329,7 @@
                     store(sib_out.at[at], prod.at[first : first + sub])
                     sib_copy(at).start()
                 for u in range(GROUP):
-                    store(own.at[slot * GROUP + u], prod.at[u * sub : (u + 1) * sub])
+                    store(own.at[(group % 2) * GROUP + u], prod.at[u * sub : (u + 1) * sub])
 
             def reduce(u, carry):
                 j = (group - 1) * GROUP + u
@@ -421,8 +424,9 @@
     drain1 = aggregate(
         0, panel1, part1, own1, tot1, sib_out1, sib_in1, hop_out1, left_in1, right_in1, finish1
     )
-    for copy in fetch(0, 0):
-        copy.start()
+    for early in range(min(SLOTS - 1, steps // GROUP)):
+        for copy in fetch(early, early):
+            copy.start()
 
     def finish2(part):
         for b in range(sub_blocks):
@@ -521,7 +525,7 @@
             pltpu.VMEM((n_row * nodes, f_in + blk), BF16),
             pltpu.VMEM((n_row * nodes, hid), BF16),
             pltpu.VMEM((col_blocks, blk, hid), BF16),
-            pltpu.VMEM((2, 2 * GROUP * sub, col_blocks * blk), BF16),
+            pltpu.VMEM((SLOTS, 2 * GROUP * sub, col_blocks * blk), BF16),
             pltpu.VMEM((2 * GROUP, sub + DEG_ROWS, f_in), F32),
             pltpu.VMEM((2 * GROUP, sub, hid), F32),
             pltpu.VMEM((sub + DEG_ROWS, f_in), F32),
@@ -533,7 +537,7 @@
         + [ring1] * 5
         + [ring2] * 5
         + [
-            pltpu.SemaphoreType.DMA((2, 2 * GROUP)),
+            pltpu.SemaphoreType.DMA((SLOTS, 2 * GROUP)),
             pltpu.SemaphoreType.DMA((3, n_row - 1, SUBS)),
             pltpu.SemaphoreType.DMA((3, n_row - 1, SUBS)),
             pltpu.SemaphoreType.DMA((2, steps)),

time: 91.9 us -> 91.9 us (level)
  no operation moved by 1% of the time
where the time goes in v5:
time: 91.9 us; the launch traced here: 91.1 us
  Pallas kernels  87.8 us (96%)
  local copies, waits for them, and re-layouts  2.6 us (3%)
    pallas_call x1, Pallas kernels, per_device(): pl.pallas_call(functools.partial(graph_kernel, n_row, n_col), out_shape=j...  75.5 us
    pallas_call x1, Pallas kernels, dense_tile(): pl.pallas_call(functools.partial(dense_kernel, part_blocks), grid=(parts,...  12.3 us
    unnamed x5, local copies, waits for them, and re-layouts  2.6 us

profile of v5, /device:TPU:0, one launch (start us, length us, event | category | flops | bytes accessed | tf_op | source)
XLA Modules:
  0.0 91.1 jit_solution(17006036600746619762)
XLA Ops:
  0.7 0.0 copy-start
  0.7 0.7 copy-done
  1.3 0.0 copy-start.1
  1.3 0.7 copy-done.1
  2.0 12.3 %dense_tile.1.a_ref = bf16[4096,2048]{1,0:T(8,128)(2,1)} custom-call(s32[1,1,192]{2,1,0:T(1,128)S(1)} %copy-done, s32[1,1,192]{2,1,0:T(1,128)S(1)} %copy-done.1, s32[1,1]{1,0:T(1,128)S(6)} %copy.14.count_ref, bf16[192,128,128]{2,1,0:T(8,128)(2,1)} %bitcast.4), custom_call_target="tpu_custom_call" | custom-call | flops 16777216 | bytes 33554432 | tf_op jit(solution)/shard_map/dense_tile/pallas_call | solution.py:64
  14.3 75.5 %graph_layers.1 = f32[4,128]{1,0:T(4,128)} custom-call(bf16[512,128]{1,0:T(8,128)(2,1)} %x_ref.1, bf16[4096,2048]{1,0:T(8,128)(2,1)} %dense_tile.1.a_ref, s32[4,4]{1,0:T(4,128)} %pair_ref.1, bf16[512,4,128]{2,1,0:T(4,128)(2,1)} %target_ref.1, bf16[128,512]{1,0:T(8,128)(2,1)} %w1_ref.1, bf16[256,512]{1,0:T(8,128)(2,1)} %bitcast.5, f32[1,256]{1,0:T(1,128)} %b2_ref.1, ...), custom_call_target="tpu_custom_call" | custom-call | tf_op jit(solution)/shard_map/graph_layers/pallas_call | solution.py:514
  89.8 1.3 %copy.15 = f32[512]{0:T(512)} copy(f32[512]{0:T(512)} %bitcast.6) | data formatting | bytes 4096
Async XLA Ops:
  0.7 0.7 copy-start
  1.3 0.7 copy-start.1

commit v6 on v2

--- a/solution.py
+++ b/solution.py
@@ -12,8 +12,9 @@
 MESH = pl.DeviceIdType.MESH
 F32 = jnp.float32
 BF16 = jnp.bfloat16
-SUBS = 4
-LAG = 2
+SUBS = 2
+LAG = 1
+OWN_LAG = 2
 DEG_ROWS = 16
 
 
@@ -155,12 +156,15 @@
     toward = jnp.where(2 * chip < chips - 1, 1, -1)
 
     def place(i):
-        r = i % chips
-        later = (r == chips - 1) & (i < steps - 1)
-        earlier = (r == 0) & (i > 0)
-        i = i + jnp.where(later, 1, 0) - jnp.where(earlier, 1, 0)
-        part = i // chips
-        s = i - part * chips
+        lag = min(OWN_LAG, chips - 1)
+        first = i < chips - 1
+        j = jnp.maximum(i - (chips - 1), 0)
+        turn = j // chips
+        r = j % chips
+        is_own = jnp.logical_not(first) & ((r == lag) | (i == steps - 1))
+        part = jnp.where(first, 0, jnp.where(is_own, turn, turn + 1))
+        later = jnp.where(is_own, chips - 1, jnp.where(r < lag, r, r - 1))
+        s = jnp.where(first, i, later)
         s2 = s - (far - near)
         paired = chip + (near - s2 // 2) * (1 - 2 * (s2 % 2))
         dest = jnp.where(s < far - near, chip + toward * (far - s), paired)
@@ -308,30 +312,44 @@
                 part, dest = place(j)
                 at = part * chips + dest
                 sib_copy(at).wait_recv()
-                tot[...] = own[j % (LAG + 1)] + sib_in[at].astype(F32)
-
-                @pl.when((dest >= chip) & has_left)
-                def _():
-                    right_copy(at, sibling).wait_recv()
-                    tot[...] += left_in[at].astype(F32)
-
-                @pl.when((dest <= chip) & has_right)
-                def _():
-                    left_copy(at, sibling).wait_recv()
-                    tot[...] += right_in[at].astype(F32)
+                mine = own.at[j % (LAG + 1)]
+
+                def forward(copy, arrived, has_up, device):
+                    @pl.when(has_up)
+                    def _():
+                        copy(at, sibling).wait_recv()
+                        hop_out[at] = (
+                            mine[...] + sib_in[at].astype(F32) + arrived[at].astype(F32)
+                        ).astype(BF16)
+
+                    @pl.when(jnp.logical_not(has_up))
+                    def _():
+                        hop_out[at] = (mine[...] + sib_in[at].astype(F32)).astype(BF16)
+
+                    copy(at, device).start()
 
                 @pl.when(dest > chip)
                 def _():
-                    hop_out[at] = tot[...].astype(BF16)
-                    right_copy(at, right).start()
+                    forward(right_copy, left_in, has_left, right)
 
                 @pl.when(dest < chip)
                 def _():
-                    hop_out[at] = tot[...].astype(BF16)
-                    left_copy(at, left).start()
+                    forward(left_copy, right_in, has_right, left)
 
                 @pl.when(dest == chip)
                 def _():
+                    tot[...] = mine[...] + sib_in[at].astype(F32)
+
+                    @pl.when(has_left)
+                    def _():
+                        right_copy(at, sibling).wait_recv()
+                        tot[...] += left_in[at].astype(F32)
+
+                    @pl.when(has_right)
+                    def _():
+                        left_copy(at, sibling).wait_recv()
+                        tot[...] += right_in[at].astype(F32)
+
                     finish(part)
 
             return carry

time: 109 us -> 89.3 us (0.82)
  Pallas kernels: 98.2 us -> 78.9 us
    pallas_call x1, Pallas kernels: 85.5 us -> 68.7 us  [per_device(): pl.pallas_call(functools.partial(graph_kernel, n_row, n_col), out_shape=j...]
    pallas_call x1, Pallas kernels: 12.7 us -> 10.2 us  [dense_tile(): pl.pallas_call(functools.partial(dense_kernel, part_blocks), grid_spec=gr...]
  transfers between devices with their start and end apart: 3 -> 3, of which waited for: 0 -> 0; matrix products, arithmetic and copies ran while one was open for 0% -> 0% of each run, Pallas kernels for 12% -> 11%
where the time goes in v6:
time: 89.3 us; the launch traced here: 88.8 us
  Pallas kernels  78.9 us (88%)
  starting transfers between devices  5.89 us (7%)
  local copies, waits for them, and re-layouts  3.3 us (4%)
    pallas_call x1, Pallas kernels, per_device(): pl.pallas_call(functools.partial(graph_kernel, n_row, n_col), out_shape=j...  68.7 us
    pallas_call x1, Pallas kernels, dense_tile(): pl.pallas_call(functools.partial(dense_kernel, part_blocks), grid_spec=gr...  10.2 us
    ppermute x3, starting transfers between devices, per_device(): lax.ppermute(attributes, 'row', [(r, (r + d) % n_row) for r in range(n_ro...  5.89 us
    unnamed x11, local copies, waits for them, and re-layouts  3.3 us
  transfers between devices with their start and end apart: 3, of which 0 were waited for; matrix products, arithmetic and copies ran while one was open for 0% of the time, Pallas kernels for 11%

profile of v6, /device:TPU:0, one launch (start us, length us, event | category | flops | bytes accessed | tf_op | source)
XLA Modules:
  0.0 88.8 jit_solution(16574690323443489747)
XLA Ops:
  0.0 3.0 %collective-permute-start.1 = (bf16[512,128]{1,0:T(8,128)(2,1)}, bf16[512,128]{1,0:T(8,128)(2,1)S(1)}, u32[]{:S(2)}, u32[]{:S(2)}) collective-permute-start(bf16[512,128]{1,0:T(8,128)(2,1)} %refs_0_.1), channel_id=1, source_target_pairs={{0,16},{8,24},{16,0},{24,8},{1,17},{9,25},{17,1},{25,9},{2,18},{10... | collective-permute-start | bytes 393224 | tf_op jit(solution)/shard_map/ppermute | solution.py:475
  3.0 1.5 %collective-permute-start = (bf16[512,128]{1,0:T(8,128)(2,1)}, bf16[512,128]{1,0:T(8,128)(2,1)S(1)}, u32[]{:S(2)}, u32[]{:S(2)}) collective-permute-start(bf16[512,128]{1,0:T(8,128)(2,1)} %refs_0_.1), channel_id=1, source_target_pairs={{0,8},{8,16},{16,24},{24,0},{1,9},{9,17},{17,25},{25,1},{2,10},{10... | collective-permute-start | bytes 393224 | tf_op jit(solution)/shard_map/ppermute | solution.py:475
  4.5 1.4 %collective-permute-start.2 = (bf16[512,128]{1,0:T(8,128)(2,1)}, bf16[512,128]{1,0:T(8,128)(2,1)S(1)}, u32[]{:S(2)}, u32[]{:S(2)}) collective-permute-start(bf16[512,128]{1,0:T(8,128)(2,1)} %refs_0_.1), channel_id=1, source_target_pairs={{0,24},{8,0},{16,8},{24,16},{1,25},{9,1},{17,9},{25,17},{2,26},{10... | collective-permute-start | bytes 393224 | tf_op jit(solution)/shard_map/ppermute | solution.py:475
  6.5 0.0 copy-start
  6.6 0.7 copy-done
  7.2 0.0 copy-start.1
  7.2 0.7 copy-done.1
  7.9 10.2 %dense_tile.1.refs_4_ = bf16[4096,2048]{1,0:T(8,128)(2,1)} custom-call(s32[192]{0:T(256)S(1)} %bitcast.8, s32[192]{0:T(256)S(1)} %bitcast.9, s32[1]{0:T(128)} %bitcast.7.count_ref, bf16[192,128,128]{2,1,0:T(8,128)(2,1)} %bitcast.10), custom_call_target="tpu_custom_call" | custom-call | flops 16777216 | bytes 33554432 | tf_op jit(solution)/shard_map/dense_tile/pallas_call | solution.py:75
  18.1 0.0 collective-permute-done.1.refs_2_
  18.1 0.0 copy-start.2
  18.1 0.0 collective-permute-done.refs_1_
  18.1 0.0 copy-start.3
  18.1 0.0 collective-permute-done.2.refs_3_
  18.1 0.0 copy-start.4
  18.1 0.6 copy-done.2
  18.7 0.0 copy-done.3
  18.8 0.0 copy-done.4
  18.8 68.7 %graph_layers.1 = f32[4,128]{1,0:T(4,128)} custom-call(bf16[512,128]{1,0:T(8,128)(2,1)} %refs_0_.1, bf16[512,128]{1,0:T(8,128)(2,1)} %copy-done.3, bf16[512,128]{1,0:T(8,128)(2,1)} %copy-done.2, bf16[512,128]{1,0:T(8,128)(2,1)} %copy-done.4, bf16[4096,2048]{1,0:T(8,128)(2,1)} %dense_tile.1.refs_4_, s32[4,4]{1,0:T(4,128)} %refs_5_.1, ...), custom_call_target="tpu_custom_call" | custom-call | tf_op jit(solution)/shard_map/graph_layers/pallas_call | solution.py:487
  87.5 1.3 %copy.15 = f32[512]{0:T(512)} copy(f32[512]{0:T(512)} %bitcast.12) | data formatting | bytes 4096
Async XLA Ops:
  0.0 18.1 %collective-permute-start.1 = (bf16[512,128]{1,0:T(8,128)(2,1)}, bf16[512,128]{1,0:T(8,128)(2,1)S(1)}, u32[]{:S(2)}, u32[]{:S(2)}) collective-permute-start(bf16[512,128]{1,0:T(8,128)(2,1)} %refs_0_.1), channel_id=1, source_target_pairs={{0,16},{8,24},{16,0},{24,8},{1,17},{9,25},{17,1},{25,9},{2,18},{10... | collective-permute-start | bytes 393224 | tf_op jit(solution)/shard_map/ppermute | solution.py:475
  3.0 15.1 %collective-permute-start = (bf16[512,128]{1,0:T(8,128)(2,1)}, bf16[512,128]{1,0:T(8,128)(2,1)S(1)}, u32[]{:S(2)}, u32[]{:S(2)}) collective-permute-start(bf16[512,128]{1,0:T(8,128)(2,1)} %refs_0_.1), channel_id=1, source_target_pairs={{0,8},{8,16},{16,24},{24,0},{1,9},{9,17},{17,25},{25,1},{2,10},{10... | collective-permute-start | bytes 393224 | tf_op jit(solution)/shard_map/ppermute | solution.py:475
  4.5 13.6 %collective-permute-start.2 = (bf16[512,128]{1,0:T(8,128)(2,1)}, bf16[512,128]{1,0:T(8,128)(2,1)S(1)}, u32[]{:S(2)}, u32[]{:S(2)}) collective-permute-start(bf16[512,128]{1,0:T(8,128)(2,1)} %refs_0_.1), channel_id=1, source_target_pairs={{0,24},{8,0},{16,8},{24,16},{1,25},{9,1},{17,9},{25,17},{2,26},{10... | collective-permute-start | bytes 393224 | tf_op jit(solution)/shard_map/ppermute | solution.py:475
  6.5 0.7 copy-start
  7.2 0.7 copy-start.1
  18.1 0.7 copy-start.2
  18.1 0.7 copy-start.3
  18.1 0.7 copy-start.4
